TPU v7x, 32 devices: a whole 2x2x4 slice. The times are simulated.
32 devices in a mesh: groups: 2 (over y), expert: 4 (over z), dp: 2 (over x), pair: 2 (over core).
Axes of the slice: x: 2, y: 2, z: 4, core: 2. Of those that a mesh axis runs over, the one named last changes fastest.
Arguments:
- tokens: bfloat16 [4096, 2048], P(('groups', 'expert', 'dp', 'pair')), parts along dimension 0, may hold values from -6 to 6
- expert_ids: int32 [4096, 2], P(('groups', 'expert', 'dp', 'pair')), parts along dimension 0, may hold values from 0 to 7, all different within a row; in each aligned block of 128 rows (0 to 127, 128 to 255, ...) at most 36 rows name the same one
- gate_weights: float32 [4096, 2], P(('groups', 'expert', 'dp', 'pair')), parts along dimension 0, may hold values from 0.1 to 1
- upstream: bfloat16 [4096, 2048], P(('groups', 'expert', 'dp', 'pair')), parts along dimension 0, may hold values from -6 to 6
- w_gate: bfloat16 [8, 2048, 1408], P(('expert', 'pair'), 'dp'), may hold values from -0.125 to 0.125
- w_up: bfloat16 [8, 2048, 1408], P(('expert', 'pair'), 'dp'), may hold values from -0.125 to 0.125
- w_down: bfloat16 [8, 1408, 2048], P(('expert', 'pair'), 'dp'), may hold values from -0.15625 to 0.15625
Outputs:
- out: bfloat16 [4096, 2048], P(('groups', 'expert', 'dp', 'pair')), parts along dimension 0
- d_tokens: bfloat16 [4096, 2048], P(('groups', 'expert', 'dp', 'pair')), parts along dimension 0
- d_gates: float32 [4096, 2], P(('groups', 'expert', 'dp', 'pair')), parts along dimension 0
- grad_gate: bfloat16 [16, 2048, 1408], P(('groups', 'expert', 'pair'), 'dp'), parts along dimension 0
- grad_up: bfloat16 [16, 2048, 1408], P(('groups', 'expert', 'pair'), 'dp'), parts along dimension 0
- grad_down: bfloat16 [16, 1408, 2048], P(('groups', 'expert', 'pair'), 'dp'), parts along dimension 0
There are 2 independent parts, one for each index of `groups`. A program takes and returns all parts, laid end to end along the dimension named above; an argument that names none is the same for every part. Nothing has to cross between parts.
Inputs may be any that keep to these rules, and one draw needn't show every extreme that they name: `expert_ids`: each token names 2 different experts; the 128 tokens of one device name one expert at most 36 times, and exactly 36 times in some blocks.
All inputs are finite; a program needn't handle non-finite values.
Results may differ from a plain program's by a relative error of at most 0.009.
Values may be sent and summed in bfloat16 or wider, within the bound.
A program may use at most 128 MiB of HBM per device.

v0:
```python
import jax
import jax.numpy as jnp
from jax import lax
from jax.sharding import PartitionSpec as P


def expert_pass(inputs, scaled, gate_w, up_w, down_w):
    gate_pre = jnp.dot(inputs, gate_w, preferred_element_type=jnp.float32)
    up_pre = jnp.dot(inputs, up_w, preferred_element_type=jnp.float32)
    squash = jax.nn.sigmoid(gate_pre)
    active = gate_pre * squash
    hidden = (active * up_pre).astype(jnp.bfloat16)
    output = jnp.dot(hidden, down_w, preferred_element_type=jnp.float32).astype(jnp.bfloat16)
    hidden_grad = lax.dot_general(
        scaled, down_w, (((1,), (1,)), ((), ())), preferred_element_type=jnp.float32
    )
    gate_grad = (hidden_grad * up_pre * (squash + active * (1.0 - squash))).astype(jnp.bfloat16)
    up_grad = (hidden_grad * active).astype(jnp.bfloat16)
    input_grad = (
        lax.dot_general(
            gate_grad, gate_w, (((1,), (1,)), ((), ())), preferred_element_type=jnp.float32
        )
        + lax.dot_general(
            up_grad, up_w, (((1,), (1,)), ((), ())), preferred_element_type=jnp.float32
        )
    ).astype(jnp.bfloat16)
    return (hidden, output, gate_grad, up_grad, input_grad)


def block_sum(first_op, second_op, n_replica):
    first_op = first_op.reshape(n_replica, -1, first_op.shape[1])
    second_op = second_op.reshape(n_replica, -1, second_op.shape[1])
    products = jnp.einsum("nsk,nsf->nkf", first_op, second_op, preferred_element_type=jnp.float32)
    rounded = lax.optimization_barrier(products.astype(jnp.bfloat16))
    return jnp.sum(rounded.astype(jnp.float32), 0).astype(jnp.bfloat16)[None]


def per_device(tokens, expert_ids, gate_weights, upstream, w_gate, w_up, w_down):
    tok_rows, model_width = tokens.shape
    chosen = expert_ids.shape[1]
    n_expert = lax.axis_size("expert")
    n_pair = lax.axis_size("pair")
    n_replica = lax.axis_size("dp")
    experts = n_expert * n_pair
    capacity = max(2, tok_rows * chosen * 9 // (experts * 8))
    row_count = tok_rows * chosen
    flat_ids = expert_ids.reshape(row_count)
    onehot = (flat_ids[:, None] == jnp.arange(experts, dtype=jnp.int32)[None, :]).astype(jnp.int32)
    position = jnp.sum(jnp.cumsum(onehot, 0) * onehot, 1) - 1
    slot_index = flat_ids * capacity + position
    source = (
        jnp.full((experts * capacity,), row_count, jnp.int32)
        .at[slot_index]
        .set(jnp.arange(row_count, dtype=jnp.int32))
    )
    zero_row = jnp.zeros((1, model_width), jnp.bfloat16)
    token_ext = jnp.concatenate([tokens, zero_row], 0)
    scaled = (gate_weights[:, :, None] * upstream.astype(jnp.float32)[:, None, :]).astype(
        jnp.bfloat16
    )
    scaled_ext = jnp.concatenate([scaled.reshape(row_count, model_width), zero_row], 0)
    send_rows = token_ext[source // chosen].reshape(experts, capacity, model_width)
    send_grads = scaled_ext[source].reshape(experts, capacity, model_width)
    full_gate, full_up, full_down = (
        lax.all_gather(w_gate, "dp", axis=1, tiled=True),
        lax.all_gather(w_up, "dp", axis=1, tiled=True),
        lax.all_gather(w_down, "dp", axis=1, tiled=True),
    )
    recv_rows, recv_grads = (
        lax.all_to_all(send_rows, ("expert", "pair"), split_axis=0, concat_axis=0, tiled=True),
        lax.all_to_all(send_grads, ("expert", "pair"), split_axis=0, concat_axis=0, tiled=True),
    )
    recv_rows = recv_rows.reshape(experts * capacity, model_width)
    recv_grads = recv_grads.reshape(experts * capacity, model_width)
    hidden, output, gate_grad, up_grad, input_grad = expert_pass(
        recv_rows, recv_grads, full_gate[0], full_up[0], full_down[0]
    )
    back_out, back_grad = (
        lax.all_to_all(
            output.reshape(experts, capacity, model_width),
            ("expert", "pair"),
            split_axis=0,
            concat_axis=0,
            tiled=True,
        ),
        lax.all_to_all(
            input_grad.reshape(experts, capacity, model_width),
            ("expert", "pair"),
            split_axis=0,
            concat_axis=0,
            tiled=True,
        ),
    )
    parts_rows, parts_hidden = (
        lax.all_to_all(recv_rows, "dp", split_axis=1, concat_axis=0, tiled=True),
        lax.all_to_all(hidden, "dp", split_axis=1, concat_axis=0, tiled=True),
    )
    all_gate, all_up, all_grads = (
        lax.all_gather(gate_grad, "dp", axis=0, tiled=True),
        lax.all_gather(up_grad, "dp", axis=0, tiled=True),
        lax.all_gather(recv_grads, "dp", axis=0, tiled=True),
    )
    grad_gate = block_sum(parts_rows, all_gate, n_replica)
    grad_up = block_sum(parts_rows, all_up, n_replica)
    grad_down = block_sum(parts_hidden, all_grads, n_replica)
    out_rows = back_out.reshape(experts * capacity, model_width)[slot_index]
    grad_rows = back_grad.reshape(experts * capacity, model_width)[slot_index]
    out_rows = out_rows.reshape(tok_rows, chosen, model_width).astype(jnp.float32)
    grad_rows = grad_rows.reshape(tok_rows, chosen, model_width).astype(jnp.float32)
    result = jnp.sum(gate_weights[:, :, None] * out_rows, 1).astype(jnp.bfloat16)
    d_gates = jnp.sum(upstream.astype(jnp.float32)[:, None, :] * out_rows, 2)
    d_tokens = jnp.sum(grad_rows, 1).astype(jnp.bfloat16)
    return (result, d_tokens, d_gates, grad_gate, grad_up, grad_down)


def solution(mesh):
    return jax.shard_map(
        per_device,
        mesh=mesh,
        in_specs=(
            P(("groups", "expert", "dp", "pair"), None),
            P(("groups", "expert", "dp", "pair"), None),
            P(("groups", "expert", "dp", "pair"), None),
            P(("groups", "expert", "dp", "pair"), None),
            P(("expert", "pair"), "dp", None),
            P(("expert", "pair"), "dp", None),
            P(("expert", "pair"), "dp", None),
        ),
        out_specs=(
            P(("groups", "expert", "dp", "pair"), None),
            P(("groups", "expert", "dp", "pair"), None),
            P(("groups", "expert", "dp", "pair"), None),
            P(("groups", "expert", "pair"), "dp", None),
            P(("groups", "expert", "pair"), "dp", None),
            P(("groups", "expert", "pair"), "dp", None),
        ),
        check_vma=False,
    )
```

profile of v0, /device:TPU:0, one launch (start us, length us, event | category | flops | bytes accessed | tf_op | source)
XLA Modules:
  0.0 402.1 jit_solution(9152714755448439231)
XLA Ops:
  12.3 2.4 mul.84
  14.7 1.8 multiply_convert_fusion
  18.7 2.4 gather_fusion.2
  22.3 6.5 %all-to-all-start.2 = ((bf16[8,36,2048]{2,1,0:T(8,128)(2,1)}), bf16[8,36,2048]{2,1,0:T(8,128)(2,1)S(1)}, u32[]{:S(2)}, u32[]{:S(2)}) async-start(bf16[8,36,2048]{2,1,0:T(8,128)(2,1)} %reshape.134), calls=%async_computation.2 | async-start | bytes 2621440 | tf_op jit(solution)/shard_map/all_to_all | solution.py:71
  28.9 3.0 gather_fusion
  31.8 2.2 reshape.130
  34.1 26.9 %all-to-all-done.2 = bf16[8,36,2048]{2,1,0:T(8,128)(2,1)S(1)} async-done(((bf16[8,36,2048]{2,1,0:T(8,128)(2,1)}), bf16[8,36,2048]{2,1,0:T(8,128)(2,1)S(1)}, u32[]{:S(2)}, u32[]{:S(2)}) %all-to-all-start.2) | async-done | bytes 1179680 | tf_op jit(solution)/shard_map/all_to_all | solution.py:71
  61.0 3.6 all-to-all-start
  65.9 30.9 %all-to-all-done = bf16[8,36,2048]{2,1,0:T(8,128)(2,1)S(1)} async-done(((bf16[8,36,2048]{2,1,0:T(8,128)(2,1)}), bf16[8,36,2048]{2,1,0:T(8,128)(2,1)S(1)}, u32[]{:S(2)}, u32[]{:S(2)}) %all-to-all-start) | async-done | bytes 1179680 | tf_op jit(solution)/shard_map/all_to_all | solution.py:70
  98.8 3.7 all-to-all-start.4
  103.8 6.2 %fusion.10 = f32[288,1408]{1,0:T(8,128)} fusion(bf16[288,2048]{1,0:T(8,128)(2,1)} %reshape.131, bf16[1,2048,1408]{2,1,0:T(8,128)(2,1)} %all-gather.7.cloned.1.call-done), kind=kOutput, calls=%fused_computation.15 | convolution fusion | flops 1660944384 | bytes 8568832 | tf_op jit(solution)/shard_map/dot_general | solution.py:8
  110.0 65.5 %all-gather.9.cloned.1.call-done = bf16[1,2048,1408]{2,1,0:T(8,128)(2,1)} async-done(((bf16[1,1024,1408]{2,1,0:T(8,128)(2,1)}), bf16[1,2048,1408]{2,1,0:T(8,128)(2,1)}) %all-gather.9.cloned.1.call-update) | async-done | bytes 5767184 | tf_op jit(solution)/shard_map/all_gather | solution.py:66
  175.5 6.2 %fusion.6 = f32[288,1408]{1,0:T(8,128)} fusion(bf16[288,2048]{1,0:T(8,128)(2,1)} %reshape.131, bf16[1,2048,1408]{2,1,0:T(8,128)(2,1)} %all-gather.9.cloned.1.call-done), kind=kOutput, calls=%fused_computation.11 | convolution fusion | flops 1660944384 | bytes 8568832 | tf_op jit(solution)/shard_map/dot_general | solution.py:9
  181.6 69.9 %all-gather.11.cloned.1.call-done = bf16[1,1408,2048]{2,1,0:T(8,128)(2,1)} async-done(((bf16[1,704,2048]{2,1,0:T(8,128)(2,1)}), bf16[1,1408,2048]{2,1,0:T(8,128)(2,1)}) %all-gather.11.cloned.1.call-update) | async-done | bytes 5767184 | tf_op jit(solution)/shard_map/all_gather | solution.py:67
  251.5 7.4 %multiply_convert_fusion.2 = (bf16[288,1408]{1,0:T(8,128)(2,1)}, bf16[288,1408]{1,0:T(8,128)(2,1)}, bf16[288,1408]{1,0:T(8,128)(2,1)}) fusion(f32[288,1408]{1,0:T(8,128)} %fusion.6, f32[288,1408]{1,0:T(8,128)} %fusion.10, bf16[288,2048]{1,0:T(8,128)(2,1)S(1)} %copy-done, bf16[1,1408,2048]{2,1,0:T(8,128)(2,1)} %all-gather.11.cloned.1.call-done), kind=kOutput, calls=%fused_computation.27 | convolution fusion | flops 1666621440 | bytes 12623872 | tf_op jit(solution)/shard_map/dot_general | solution.py:14
  258.9 2.9 all_to_all.43
  262.8 6.4 %fusion.4 = f32[288,2048]{1,0:T(8,128)} fusion(bf16[288,1408]{1,0:T(8,128)(2,1)} %get-tuple-element.16, bf16[1,2048,1408]{2,1,0:T(8,128)(2,1)} %all-gather.9.cloned.1.call-done), kind=kOutput, calls=%fused_computation.9 | convolution fusion | flops 1660944384 | bytes 8937472 | tf_op jit(solution)/shard_map/dot_general | solution.py:23
  269.2 4.3 %all-to-all-start.5 = ((bf16[288,2,704]{2,0,1:T(8,128)(2,1)}), bf16[288,2,704]{2,0,1:T(8,128)(2,1)}, u32[]{:S(2)}, u32[]{:S(2)}) async-start(bf16[288,2,704]{2,0,1:T(8,128)(2,1)} %copy.28), calls=%async_computation.5 | async-start | bytes 1769472 | tf_op jit(solution)/shard_map/all_to_all | solution.py:96
  273.5 5.6 %fusion.18 = bf16[288,2048]{1,0:T(8,128)(2,1)S(1)} fusion(f32[288,2048]{1,0:T(8,128)} %fusion.4, bf16[288,1408]{1,0:T(8,128)(2,1)} %get-tuple-element.14, bf16[1,2048,1408]{2,1,0:T(8,128)(2,1)} %all-gather.7.cloned.1.call-done), kind=kOutput, calls=%fused_computation.22 | convolution fusion | flops 1662124032 | bytes 10117120 | tf_op jit(solution)/shard_map/dot_general | solution.py:20
  280.3 15.6 %all-to-all-done.5 = bf16[288,2,704]{2,0,1:T(8,128)(2,1)} async-done(((bf16[288,2,704]{2,0,1:T(8,128)(2,1)}), bf16[288,2,704]{2,0,1:T(8,128)(2,1)}, u32[]{:S(2)}, u32[]{:S(2)}) %all-to-all-start.5) | async-done | bytes 811040 | tf_op jit(solution)/shard_map/all_to_all | solution.py:96
  295.9 4.7 %all-to-all-start.3 = ((bf16[8,36,2048]{2,1,0:T(8,128)(2,1)}), bf16[8,36,2048]{2,1,0:T(8,128)(2,1)S(1)}, u32[]{:S(2)}, u32[]{:S(2)}) async-start(bf16[8,36,2048]{2,1,0:T(8,128)(2,1)} %reshape.136), calls=%async_computation.3 | async-start | bytes 2621440 | tf_op jit(solution)/shard_map/all_to_all | solution.py:86
  301.2 4.9 %fusion.15 = bf16[288,2048]{1,0:T(8,128)(2,1)S(1)} fusion(bf16[288,1408]{1,0:T(8,128)(2,1)} %get-tuple-element.15, bf16[1,1408,2048]{2,1,0:T(8,128)(2,1)} %all-gather.11.cloned.1.call-done), kind=kOutput, calls=%fused_computation.21 | convolution fusion | flops 1661534208 | bytes 7757824 | tf_op jit(solution)/shard_map/dot_general | solution.py:13
  307.3 25.5 %all-to-all-done.3 = bf16[8,36,2048]{2,1,0:T(8,128)(2,1)S(1)} async-done(((bf16[8,36,2048]{2,1,0:T(8,128)(2,1)}), bf16[8,36,2048]{2,1,0:T(8,128)(2,1)S(1)}, u32[]{:S(2)}, u32[]{:S(2)}) %all-to-all-start.3) | async-done | bytes 1179680 | tf_op jit(solution)/shard_map/all_to_all | solution.py:86
  332.8 4.5 %all-to-all-start.1 = ((bf16[8,36,2048]{2,1,0:T(8,128)(2,1)}), bf16[8,36,2048]{2,1,0:T(8,128)(2,1)}, u32[]{:S(2)}, u32[]{:S(2)}) async-start(bf16[8,36,2048]{2,1,0:T(8,128)(2,1)} %reshape.132), calls=%async_computation.1 | async-start | bytes 2621440 | tf_op jit(solution)/shard_map/all_to_all | solution.py:79
  338.4 7.6 %convolution_convert_fusion.2 = bf16[2,704,2048]{2,1,0:T(8,128)(2,1)} fusion(bf16[2,288,2048]{2,1,0:T(8,128)(2,1)} %bitcast.60, bf16[288,2,704]{2,0,1:T(8,128)(2,1)} %all-to-all-done.5), kind=kOutput, calls=%fused_computation.19 | convolution fusion | flops 1663827968 | bytes 8937472 | tf_op jit(solution)/shard_map/nsk,nsf->nkf/dot_general | solution.py:33
  346.1 6.4 %reduce_sum.81 = bf16[704,2048]{1,0:T(8,128)(2,1)} reduce(bf16[2,704,2048]{2,1,0:T(8,128)(2,1)} %convolution_convert_fusion.2, bf16[]{:T(256)} %constant.32.clone.1), dimensions={0}, to_apply=%region_9.10 | reduce | flops 1441792 | bytes 8650754 | tf_op jit(solution)/shard_map/reduce_sum | solution.py:35
  352.5 6.6 %convolution_convert_fusion = bf16[2,1024,1408]{2,1,0:T(8,128)(2,1)} fusion(bf16[2,288,1408]{2,1,0:T(8,128)(2,1)} %bitcast.61, bf16[288,2,1024]{2,0,1:T(8,128)(2,1)S(1)} %copy-done.3), kind=kOutput, calls=%fused_computation.17 | convolution fusion | flops 1663827968 | bytes 8568832 | tf_op jit(solution)/shard_map/nsk,nsf->nkf/dot_general | solution.py:33
  359.1 6.1 %reduce_sum.80 = bf16[1024,1408]{1,0:T(8,128)(2,1)} reduce(bf16[2,1024,1408]{2,1,0:T(8,128)(2,1)} %convolution_convert_fusion, bf16[]{:T(256)} %constant.32.clone.1), dimensions={0}, to_apply=%region_8.9 | reduce | flops 1441792 | bytes 8650754 | tf_op jit(solution)/shard_map/reduce_sum | solution.py:35
  365.2 6.8 %convolution_convert_fusion.1 = bf16[2,1024,1408]{2,1,0:T(8,128)(2,1)} fusion(bf16[2,288,1408]{2,1,0:T(8,128)(2,1)} %bitcast.62, bf16[288,2,1024]{2,0,1:T(8,128)(2,1)S(1)} %copy-done.3), kind=kOutput, calls=%fused_computation.18 | convolution fusion | flops 1663827968 | bytes 8568832 | tf_op jit(solution)/shard_map/nsk,nsf->nkf/dot_general | solution.py:33
  372.0 6.1 %reduce_sum.79 = bf16[1024,1408]{1,0:T(8,128)(2,1)} reduce(bf16[2,1024,1408]{2,1,0:T(8,128)(2,1)} %convolution_convert_fusion.1, bf16[]{:T(256)} %constant.32.clone.1), dimensions={0}, to_apply=%region_7.8 | reduce | flops 1441792 | bytes 8650754 | tf_op jit(solution)/shard_map/reduce_sum | solution.py:35
  380.5 3.6 reduce_sum.77
  388.2 6.0 %multiply_reduce_fusion = (f32[128,2]{1,0:T(8,128)S(1)}, bf16[128,2048]{1,0:T(8,128)(2,1)}) fusion(f32[128,2,2048]{2,1,0:T(2,128)S(1)} %reshape.142, f32[128,2048]{1,0:T(8,128)} %convert_element_type.64, f32[128,2]{1,0:T(8,128)S(1)} %copy.22), kind=kLoop, calls=%fused_computation.23 | loop fusion | flops 1834752 | bytes 3672064 | tf_op jit(solution)/shard_map/reduce_sum | solution.py:111
  (75 shorter events, 25.2 us)
Async XLA Ops:
  7.2 96.7 %all-gather.7.cloned.1.call-start = ((), (), s32[]{:S(2)}) async-start(), calls=%async_computation.6 | async-start | bytes 8650752 | tf_op jit(solution)/shard_map/all_gather | solution.py:65
  7.9 167.6 %all-gather.9.cloned.1.call-start = ((), (), s32[]{:S(2)}) async-start(), calls=%async_computation.7 | async-start | bytes 8650752 | tf_op jit(solution)/shard_map/all_gather | solution.py:66
  8.7 0.8 copy-start.6
  8.7 2.3 copy-start.7
  8.7 2.5 copy-start.1
  8.7 242.9 %all-gather.11.cloned.1.call-start = ((), (), s32[]{:S(2)}) async-start(), calls=%async_computation.8 | async-start | bytes 8650752 | tf_op jit(solution)/shard_map/all_gather | solution.py:67
  10.7 4.0 %copy-start.5 = (s32[8,3]{0,1:T(4,128)}, s32[8,3]{0,1:T(4,128)S(1)}, u32[]{:S(2)}) copy-start(s32[8,3]{0,1:T(4,128)S(1)} %reduce-window.9) | copy-start | bytes 292
  16.5 0.7 slice-start
  22.3 6.5 %copy-start.4 = (bf16[128,2048]{1,0:T(8,128)(2,1)S(1)}, bf16[128,2048]{1,0:T(8,128)(2,1)}, u32[]{:S(2)}) copy-start(bf16[128,2048]{1,0:T(8,128)(2,1)} %param.7) | copy-start | bytes 1572868
  22.3 38.7 %all-to-all-start.2 = ((bf16[8,36,2048]{2,1,0:T(8,128)(2,1)}), bf16[8,36,2048]{2,1,0:T(8,128)(2,1)S(1)}, u32[]{:S(2)}, u32[]{:S(2)}) async-start(bf16[8,36,2048]{2,1,0:T(8,128)(2,1)} %reshape.134), calls=%async_computation.2 | async-start | bytes 2621440 | tf_op jit(solution)/shard_map/all_to_all | solution.py:71
  61.0 35.7 %all-to-all-start = ((bf16[8,36,2048]{2,1,0:T(8,128)(2,1)}), bf16[8,36,2048]{2,1,0:T(8,128)(2,1)S(1)}, u32[]{:S(2)}, u32[]{:S(2)}) async-start(bf16[8,36,2048]{2,1,0:T(8,128)(2,1)} %reshape.130), calls=%async_computation | async-start | bytes 2621440 | tf_op jit(solution)/shard_map/all_to_all | solution.py:70
  64.6 273.8 %all-gather.17.cloned.1.call-start = ((), (), s32[]{:S(2)}) async-start(), calls=%async_computation.11 | async-start | bytes 3538944 | tf_op jit(solution)/shard_map/all_gather | solution.py:101
  98.8 170.4 %all-to-all-start.4 = ((bf16[288,2,1024]{2,0,1:T(8,128)(2,1)}), bf16[288,2,1024]{2,0,1:T(8,128)(2,1)S(1)}, u32[]{:S(2)}, u32[]{:S(2)}) async-start(bf16[288,2,1024]{2,0,1:T(8,128)(2,1)} %copy.27), calls=%async_computation.4 | async-start | bytes 2359296 | tf_op jit(solution)/shard_map/all_to_all | solution.py:95
  102.5 250.0 %all-gather.15.cloned.1.call-start = ((), (), s32[]{:S(2)}) async-start(), calls=%async_computation.10 | async-start | bytes 2433024 | tf_op jit(solution)/shard_map/all_gather | solution.py:100
  110.0 141.5 %copy-start = (bf16[288,2048]{1,0:T(8,128)(2,1)S(1)}, bf16[288,2048]{1,0:T(8,128)(2,1)}, u32[]{:S(2)}) copy-start(bf16[288,2048]{1,0:T(8,128)(2,1)} %reshape.135) | copy-start | bytes 3538948
  269.2 10.0 %copy-start.2 = (bf16[288,2,1024]{2,0,1:T(8,128)(2,1)}, bf16[288,2,1024]{2,0,1:T(8,128)(2,1)S(1)}, u32[]{:S(2)}) copy-start(bf16[288,2,1024]{2,0,1:T(8,128)(2,1)S(1)} %all-to-all-done.4) | copy-start | bytes 3538948
  269.2 26.8 %all-to-all-start.5 = ((bf16[288,2,704]{2,0,1:T(8,128)(2,1)}), bf16[288,2,704]{2,0,1:T(8,128)(2,1)}, u32[]{:S(2)}, u32[]{:S(2)}) async-start(bf16[288,2,704]{2,0,1:T(8,128)(2,1)} %copy.28), calls=%async_computation.5 | async-start | bytes 1769472 | tf_op jit(solution)/shard_map/all_to_all | solution.py:96
  295.9 36.9 %all-to-all-start.3 = ((bf16[8,36,2048]{2,1,0:T(8,128)(2,1)}), bf16[8,36,2048]{2,1,0:T(8,128)(2,1)S(1)}, u32[]{:S(2)}, u32[]{:S(2)}) async-start(bf16[8,36,2048]{2,1,0:T(8,128)(2,1)} %reshape.136), calls=%async_computation.3 | async-start | bytes 2621440 | tf_op jit(solution)/shard_map/all_to_all | solution.py:86
  300.6 64.5 %all-gather.13.cloned.1.call-start = ((), (), s32[]{:S(2)}) async-start(), calls=%async_computation.9 | async-start | bytes 2433024 | tf_op jit(solution)/shard_map/all_gather | solution.py:99
  332.8 51.3 %all-to-all-start.1 = ((bf16[8,36,2048]{2,1,0:T(8,128)(2,1)}), bf16[8,36,2048]{2,1,0:T(8,128)(2,1)}, u32[]{:S(2)}, u32[]{:S(2)}) async-start(bf16[8,36,2048]{2,1,0:T(8,128)(2,1)} %reshape.132), calls=%async_computation.1 | async-start | bytes 2621440 | tf_op jit(solution)/shard_map/all_to_all | solution.py:79
  346.1 6.4 %copy-start.3 = (bf16[288,2,1024]{2,0,1:T(8,128)(2,1)S(1)}, bf16[288,2,1024]{2,0,1:T(8,128)(2,1)}, u32[]{:S(2)}) copy-start(bf16[288,2,1024]{2,0,1:T(8,128)(2,1)} %copy-done.2) | copy-start | bytes 3538948
Sparse Core Ops, SparseCore 0:
  9.5 77.1 all-gather.6
  88.3 87.1 all-gather.8
  177.0 74.4 all-gather.10
  252.9 45.5 all-gather.16
  299.9 27.7 all-gather.14
  329.1 27.7 all-gather.12
where the time goes:
time: 408 us; the launch traced here: 402 us
  waiting for transfers between devices  237 us (58%)
  matrix products  57.6 us (14%)
  local copies, waits for them, and re-layouts  33.3 us (8%)
  other arithmetic  31.8 us (8%)
  starting transfers between devices  27.6 us (7%)
  between operations  14.8 us (4%)
    all_gather x1, waiting for transfers between devices, per_device(): lax.all_gather(w_down, 'dp', axis=1, tiled=True)  69.9 us
    all_gather x1, waiting for transfers between devices, per_device(): lax.all_gather(w_up, 'dp', axis=1, tiled=True)  65.5 us
    all_to_all x1, waiting for transfers between devices, per_device(): lax.all_to_all(send_rows, ('expert', 'pair'), split_axis=0, concat_axis=0...  30.9 us
    all_to_all x1, waiting for transfers between devices, per_device(): lax.all_to_all(send_grads, ('expert', 'pair'), split_axis=0, concat_axis=...  26.9 us
    all_to_all x1, waiting for transfers between devices, per_device(): lax.all_to_all(input_grad.reshape(experts, capacity, model_width), ('expe...  25.5 us
    dot_general x3, matrix products, block_sum(): jnp.einsum('nsk,nsf->nkf', first_op, second_op, preferred_element_type=jn...  21 us
    reduce_sum x3, other arithmetic, block_sum(): return jnp.sum(rounded.astype(jnp.float32), 0).astype(jnp.bfloat16)[None]  18.6 us
    all_to_all x1, waiting for transfers between devices, per_device(): lax.all_to_all(hidden, 'dp', split_axis=1, concat_axis=0, tiled=True)  15.6 us
  transfers between devices with their start and end apart: 12, of which 6 were waited for; matrix products, arithmetic and copies ran while one was open for 27% of the time, Pallas kernels for 0%

commit v1 on v0

v1 whole, which is shorter than its diff:
```python
import jax
import jax.numpy as jnp
from jax import lax
from jax.sharding import PartitionSpec as P

F32 = jnp.float32
BF16 = jnp.bfloat16


def shift(value, axis, step):
    size = lax.axis_size(axis)
    return lax.ppermute(value, axis, [(i, (i + step) % size) for i in range(size)])


def gather_weight(weight):
    rows, cols = weight.shape
    n_replica = lax.axis_size("dp")
    n_group = lax.axis_size("groups")
    me = lax.axis_index("dp")
    group = lax.axis_index("groups")
    if rows % (16 * n_group):
        n_group, group = 1, 0
    share = rows // n_group
    mine = lax.dynamic_slice_in_dim(weight, group * share, share, 0)
    full = jnp.zeros((n_replica * rows, cols), weight.dtype)
    full = lax.dynamic_update_slice_in_dim(full, weight, me * rows, 0)
    for step in range(1, n_replica):
        owner = lax.rem(me - step + n_replica, n_replica)
        piece = shift(mine, "dp", step)
        full = lax.dynamic_update_slice_in_dim(full, piece, owner * rows + group * share, 0)
        for hop in range(1, n_group):
            other = shift(piece, "groups", hop)
            origin = lax.rem(group - hop + n_group, n_group)
            full = lax.dynamic_update_slice_in_dim(full, other, owner * rows + origin * share, 0)
    return full


def dot(a, b, a_dim=1, b_dim=0):
    return lax.dot_general(a, b, (((a_dim,), (b_dim,)), ((), ())), preferred_element_type=F32)


def per_device(tokens, expert_ids, gate_weights, upstream, w_gate, w_up, w_down):
    tok_rows, model_width = tokens.shape
    chosen = expert_ids.shape[1]
    n_expert = lax.axis_size("expert")
    n_pair = lax.axis_size("pair")
    n_replica = lax.axis_size("dp")
    me = lax.axis_index("dp")
    experts = n_expert * n_pair
    capacity = max(2, tok_rows * chosen * 9 // (experts * 8))
    row_count = tok_rows * chosen
    slots = experts * capacity

    full_gate = gather_weight(w_gate[0])
    full_up = gather_weight(w_up[0])
    full_down = gather_weight(w_down[0])

    flat_ids = expert_ids.reshape(row_count)
    order = jnp.arange(row_count, dtype=jnp.int32)
    same = (flat_ids[:, None] == flat_ids[None, :]) & (order[None, :] < order[:, None])
    position = jnp.sum(same.astype(jnp.int32), 1)
    slot_index = (flat_ids * capacity + position).reshape(tok_rows, chosen)
    slot_ids = jnp.arange(slots, dtype=jnp.int32)
    picks = [(slot_ids[:, None] == slot_index[None, :, k]).astype(BF16) for k in range(chosen)]
    any_pick = sum(picks[1:], picks[0])
    wide = upstream.astype(F32)
    send_rows = dot(any_pick, tokens).astype(BF16)
    send_grads = sum(
        dot(picks[k], (gate_weights[:, k : k + 1] * wide).astype(BF16)) for k in range(chosen)
    ).astype(BF16)

    def exchange(value):
        value = value.reshape(experts, capacity, model_width)
        value = lax.all_to_all(value, ("expert", "pair"), split_axis=0, concat_axis=0, tiled=True)
        return value.reshape(slots, model_width)

    rows = exchange(send_rows)
    grads = exchange(send_grads)
    gate_pre = dot(rows, full_gate)
    up_pre = dot(rows, full_up)
    squash = jax.nn.sigmoid(gate_pre)
    active = gate_pre * squash
    hidden = (active * up_pre).astype(BF16)
    output = dot(hidden, full_down).astype(BF16)
    back_out = exchange(output)
    hidden_grad = dot(grads, full_down, 1, 1)
    gate_grad = (hidden_grad * up_pre * (squash + active * (1.0 - squash))).astype(BF16)
    up_grad = (hidden_grad * active).astype(BF16)
    input_grad = (dot(gate_grad, full_gate, 1, 1) + dot(up_grad, full_up, 1, 1)).astype(BF16)
    back_grad = exchange(input_grad)

    def part(value, index):
        width = value.shape[1] // n_replica
        return lax.dynamic_slice_in_dim(value, index * width, width, 1)

    sum_gate = dot(part(rows, me), gate_grad, 0, 0)
    sum_up = dot(part(rows, me), up_grad, 0, 0)
    sum_down = dot(part(hidden, me), grads, 0, 0)
    for step in range(1, n_replica):
        target = lax.rem(me + step, n_replica)
        their_grads = shift(grads, "dp", step)
        their_rows = shift(part(rows, target), "dp", step)
        their_hidden = shift(part(hidden, target), "dp", step)
        their_gate = shift(gate_grad, "dp", step)
        their_up = shift(up_grad, "dp", step)
        sum_down += dot(their_hidden, their_grads, 0, 0)
        sum_gate += dot(their_rows, their_gate, 0, 0)
        sum_up += dot(their_rows, their_up, 0, 0)

    out_rows = [dot(picks[k], back_out, 0, 0) for k in range(chosen)]
    result = sum(gate_weights[:, k : k + 1] * out_rows[k] for k in range(chosen)).astype(BF16)
    d_gates = jnp.stack([jnp.sum(wide * out_rows[k], 1) for k in range(chosen)], 1)
    d_tokens = dot(any_pick, back_grad, 0, 0).astype(BF16)
    return (
        result,
        d_tokens,
        d_gates,
        sum_gate.astype(BF16)[None],
        sum_up.astype(BF16)[None],
        sum_down.astype(BF16)[None],
    )


def solution(mesh):
    rows = P(("groups", "expert", "dp", "pair"), None)
    weights = P(("expert", "pair"), "dp", None)
    summed = P(("groups", "expert", "pair"), "dp", None)
    return jax.shard_map(
        per_device,
        mesh=mesh,
        in_specs=(rows, rows, rows, rows, weights, weights, weights),
        out_specs=(rows, rows, rows, summed, summed, summed),
        check_vma=False,
    )
```

time: 408 us -> 250 us (0.61); the launches traced: 402 us -> 249 us
  waiting for transfers between devices: 237 us -> 96.3 us
  other arithmetic: 31.8 us -> 1.46 us
  between operations: 14.8 us -> 0.91 us
  local copies, waits for them, and re-layouts: 33.3 us -> 46.6 us
  matrix products: 57.6 us -> 70.2 us
  starting transfers between devices: 27.6 us -> 33.1 us
    all_gather x6 -> x0, waiting for transfers between devices: 135 us -> none  [the longest x1 69.9 us: per_device(): lax.all_gather(w_down, 'dp', axis=1, tiled=True)]
    all_to_all x6 -> x4, waiting for transfers between devices: 98.9 us -> 33.9 us  [exchange(): lax.all_to_all(value, ('expert', 'pair'), split_axis=0, concat_axis=0, ti...]
    ppermute x0 -> x11, waiting for transfers between devices: none -> 62.4 us  [shift(): lax.ppermute(value, axis, [(i, (i + step) % size) for i in range(size)])]
    reduce_sum x6 -> x1, other arithmetic: 28.3 us -> 0.18 us  [per_device(): position = jnp.sum(same.astype(jnp.int32), 1)]
    dynamic_update_slice x0 -> x9, local copies, waits for them, and re-layouts: none -> 19.7 us  [the longest x3 7.84 us: gather_weight(): lax.dynamic_update_slice_in_dim(full, other, owner * rows + origin * shar...]
    ppermute x0 -> x11, starting transfers between devices: none -> 13.6 us  [shift(): lax.ppermute(value, axis, [(i, (i + step) % size) for i in range(size)])]
    dot_general x9 -> x18, matrix products: 57.6 us -> 70.2 us  [dot(): lax.dot_general(a, b, (((a_dim,), (b_dim,)), ((), ())), preferred_element...]
    gather x4 -> x0, local copies, waits for them, and re-layouts: 8.13 us -> none  [the longest x1 2.97 us: per_device(): token_ext[source // chosen].reshape(experts, capacity, model_width)]
  transfers between devices with their start and end apart: 12 -> 15, of which waited for: 6 -> 7; matrix products, arithmetic and copies ran while one was open for 27% -> 43% of each run, Pallas kernels for 0% -> 0%
where the time goes in v1:
time: 250 us; the launch traced here: 249 us
  waiting for transfers between devices  96.3 us (39%)
  matrix products  70.2 us (28%)
  local copies, waits for them, and re-layouts  46.6 us (19%)
  starting transfers between devices  33.1 us (13%)
    dot_general x18, matrix products, dot(): lax.dot_general(a, b, (((a_dim,), (b_dim,)), ((), ())), preferred_element...  70.2 us
    ppermute x11, waiting for transfers between devices, shift(): lax.ppermute(value, axis, [(i, (i + step) % size) for i in range(size)])  62.4 us
    all_to_all x4, waiting for transfers between devices, exchange(): lax.all_to_all(value, ('expert', 'pair'), split_axis=0, concat_axis=0, ti...  33.9 us
    all_to_all x4, starting transfers between devices, exchange(): lax.all_to_all(value, ('expert', 'pair'), split_axis=0, concat_axis=0, ti...  19.5 us
    ppermute x11, starting transfers between devices, shift(): lax.ppermute(value, axis, [(i, (i + step) % size) for i in range(size)])  13.6 us
    dynamic_update_slice x3, local copies, waits for them, and re-layouts, gather_weight(): lax.dynamic_update_slice_in_dim(full, other, owner * rows + origin * shar...  7.84 us
    dynamic_update_slice x3, local copies, waits for them, and re-layouts, gather_weight(): lax.dynamic_update_slice_in_dim(full, piece, owner * rows + group * share...  7.81 us
    reshape x4, local copies, waits for them, and re-layouts, exchange(): value = value.reshape(experts, capacity, model_width)  6.03 us
  transfers between devices with their start and end apart: 15, of which 7 were waited for; matrix products, arithmetic and copies ran while one was open for 43% of the time, Pallas kernels for 0%

profile of v1, /device:TPU:0, one launch (start us, length us, event | category | flops | bytes accessed | tf_op | source)
XLA Modules:
  0.0 248.6 jit_solution(13453924309039697237)
XLA Ops:
  6.7 6.3 %all-to-all-start = ((bf16[8,36,2048]{2,1,0:T(8,128)(2,1)}), bf16[8,36,2048]{2,1,0:T(8,128)(2,1)}, u32[]{:S(2)}, u32[]{:S(2)}) async-start(bf16[8,36,2048]{2,1,0:T(8,128)(2,1)} %reshape.46), calls=%async_computation | async-start | bytes 2621440 | tf_op jit(solution)/shard_map/all_to_all | solution.py:74
  18.0 2.6 %dynamic-slice_bitcast_fusion = bf16[352,2048]{1,0:T(8,128)(2,1)} fusion(bf16[1,704,2048]{2,1,0:T(8,128)(2,1)} %param.13, s32[]{:T(128)S(6)} %select_n.42), kind=kLoop, calls=%fused_computation.24 | loop fusion | bytes 2883588 | tf_op jit(solution)/shard_map/dynamic_slice | solution.py:24
  27.5 17.8 %all-to-all-done = bf16[8,36,2048]{2,1,0:T(8,128)(2,1)} async-done(((bf16[8,36,2048]{2,1,0:T(8,128)(2,1)}), bf16[8,36,2048]{2,1,0:T(8,128)(2,1)}, u32[]{:S(2)}, u32[]{:S(2)}) %all-to-all-start) | async-done | bytes 1179680 | tf_op jit(solution)/shard_map/all_to_all | solution.py:74
  45.3 3.8 %all-to-all-start.2 = ((bf16[8,36,2048]{2,1,0:T(8,128)(2,1)}), bf16[8,36,2048]{2,1,0:T(8,128)(2,1)S(1)}, u32[]{:S(2)}, u32[]{:S(2)}) async-start(bf16[8,36,2048]{2,1,0:T(8,128)(2,1)} %reshape.50), calls=%async_computation.2 | async-start | bytes 2621440 | tf_op jit(solution)/shard_map/all_to_all | solution.py:74
  49.1 2.9 %broadcast.10.clone.1 = bf16[2048,1408]{1,0:T(8,128)(2,1)} broadcast(bf16[]{:T(256)} %constant.35.clone.1), dimensions={} | broadcast | bytes 5767170 | tf_op jit(solution)/shard_map/broadcast.3
  55.3 24.5 %collective-permute-done = bf16[512,1408]{1,0:T(8,128)(2,1)} collective-permute-done((bf16[512,1408]{1,0:T(8,128)(2,1)}, bf16[512,1408]{1,0:T(8,128)(2,1)}, u32[]{:S(2)}, u32[]{:S(2)}) %collective-permute-start) | collective-permute-done | bytes 1441824 | tf_op jit(solution)/shard_map/ppermute | solution.py:12
  81.3 3.2 %broadcast_in_dim.16 = bf16[1408,2048]{1,0:T(8,128)(2,1)} broadcast(bf16[]{:T(256)} %constant.35.clone.1), dimensions={} | broadcast | bytes 5767170 | tf_op jit(solution)/shard_map/broadcast_in_dim | solution.py:25
  86.3 24.0 %collective-permute-done.4 = bf16[352,2048]{1,0:T(8,128)(2,1)} collective-permute-done((bf16[352,2048]{1,0:T(8,128)(2,1)}, bf16[352,2048]{1,0:T(8,128)(2,1)}, u32[]{:S(2)}, u32[]{:S(2)}) %collective-permute-start.4) | collective-permute-done | bytes 1441824 | tf_op jit(solution)/shard_map/ppermute | solution.py:12
  111.8 2.7 %constant_dynamic-update-slice_fusion.1 = bf16[1408,2048]{1,0:T(8,128)(2,1)} fusion(bf16[1408,2048]{1,0:T(8,128)(2,1)} %bitcast_dynamic-update-slice_fusion, bf16[352,2048]{1,0:T(8,128)(2,1)} %collective-permute-done.4, s32[]{:T(128)S(6)} %select_n.43), kind=kLoop, calls=%fused_computation.66 | loop fusion | bytes 2883588 | tf_op jit(solution)/shard_map/dynamic_update_slice | solution.py:30
  117.0 2.6 %constant_dynamic-update-slice_fusion.5 = bf16[2048,1408]{1,0:T(8,128)(2,1)} fusion(bf16[2048,1408]{1,0:T(8,128)(2,1)} %bitcast_dynamic-update-slice_fusion.2, bf16[512,1408]{1,0:T(8,128)(2,1)} %collective-permute-done, s32[]{:T(128)S(6)} %select_n.39), kind=kLoop, calls=%fused_computation.70 | loop fusion | bytes 2883588 | tf_op jit(solution)/shard_map/dynamic_update_slice | solution.py:30
  125.2 2.6 %constant_dynamic-update-slice_fusion.2 = bf16[2048,1408]{1,0:T(8,128)(2,1)} fusion(bf16[2048,1408]{1,0:T(8,128)(2,1)} %constant_dynamic-update-slice_fusion.3, bf16[512,1408]{1,0:T(8,128)(2,1)} %collective-permute-done.3, s32[]{:T(128)S(6)} %select_n.40), kind=kLoop, calls=%fused_computation.67 | loop fusion | bytes 2883588 | tf_op jit(solution)/shard_map/dynamic_update_slice | solution.py:34
  127.7 2.6 %constant_dynamic-update-slice_fusion.4 = bf16[2048,1408]{1,0:T(8,128)(2,1)} fusion(bf16[2048,1408]{1,0:T(8,128)(2,1)} %constant_dynamic-update-slice_fusion.5, bf16[512,1408]{1,0:T(8,128)(2,1)} %collective-permute-done.1, s32[]{:T(128)S(6)} %select_n.40), kind=kLoop, calls=%fused_computation.69 | loop fusion | bytes 2883588 | tf_op jit(solution)/shard_map/dynamic_update_slice | solution.py:34
  130.3 4.6 %fusion.41 = f32[288,1408]{1,0:T(8,128)S(1)} fusion(bf16[288,2048]{1,0:T(8,128)(2,1)S(1)} %reshape.47, bf16[2048,1408]{1,0:T(8,128)(2,1)} %constant_dynamic-update-slice_fusion.2), kind=kOutput, calls=%fused_computation.78 | convolution fusion | flops 1660944384 | bytes 8568832 | tf_op jit(solution)/shard_map/dot_general | solution.py:39
  134.9 4.6 %fusion.40 = f32[288,1408]{1,0:T(8,128)S(1)} fusion(bf16[288,2048]{1,0:T(8,128)(2,1)S(1)} %reshape.47, bf16[2048,1408]{1,0:T(8,128)(2,1)} %constant_dynamic-update-slice_fusion.4), kind=kOutput, calls=%fused_computation.77 | convolution fusion | flops 1660944384 | bytes 8568832 | tf_op jit(solution)/shard_map/dot_general | solution.py:39
  139.6 10.0 %collective-permute-done.5 = bf16[352,2048]{1,0:T(8,128)(2,1)} collective-permute-done((bf16[352,2048]{1,0:T(8,128)(2,1)}, bf16[352,2048]{1,0:T(8,128)(2,1)}, u32[]{:S(2)}, u32[]{:S(2)}) %collective-permute-start.5) | collective-permute-done | bytes 1441824 | tf_op jit(solution)/shard_map/ppermute | solution.py:12
  149.6 2.7 %constant_dynamic-update-slice_fusion = bf16[1408,2048]{1,0:T(8,128)(2,1)} fusion(bf16[1408,2048]{1,0:T(8,128)(2,1)} %constant_dynamic-update-slice_fusion.1, bf16[352,2048]{1,0:T(8,128)(2,1)} %collective-permute-done.5, s32[]{:T(128)S(6)} %select_n.44), kind=kLoop, calls=%fused_computation.65 | loop fusion | bytes 2883588 | tf_op jit(solution)/shard_map/dynamic_update_slice | solution.py:34
  152.3 6.4 %multiply_convert_fusion.1 = (bf16[288,1408]{1,0:T(8,128)(2,1)}, bf16[288,1408]{1,0:T(8,128)(2,1)S(1)}, bf16[288,1408]{1,0:T(8,128)(2,1)}) fusion(f32[288,1408]{1,0:T(8,128)S(1)} %fusion.41, f32[288,1408]{1,0:T(8,128)S(1)} %fusion.40, bf16[288,2048]{1,0:T(8,128)(2,1)S(1)} %copy-done.7, bf16[1408,2048]{1,0:T(8,128)(2,1)} %constant_dynamic-update-slice_fusion), kind=kOutput, calls=%fused_computation.21 | convolution fusion | flops 1666621440 | bytes 12623872 | tf_op jit(solution)/shard_map/dot_general | solution.py:39
  158.7 5.7 %fusion.17 = f32[1024,1408]{1,0:T(8,128)} fusion(bf16[288,1408]{1,0:T(8,128)(2,1)} %get-tuple-element.8, bf16[288,2048]{1,0:T(8,128)(2,1)S(1)} %reshape.47, s32[]{:T(128)S(6)} %select_n.37), kind=kOutput, calls=%fused_computation.38 | convolution fusion | flops 830472192 | bytes 7168004 | tf_op jit(solution)/shard_map/dot_general | solution.py:39
  165.8 4.7 %convolution_convert_fusion.1 = bf16[288,2048]{1,0:T(8,128)(2,1)S(1)} fusion(bf16[288,1408]{1,0:T(8,128)(2,1)S(1)} %get-tuple-element.9, bf16[1408,2048]{1,0:T(8,128)(2,1)} %constant_dynamic-update-slice_fusion), kind=kOutput, calls=%fused_computation.13 | convolution fusion | flops 1661534208 | bytes 7757824 | tf_op jit(solution)/shard_map/dot_general | solution.py:39
  171.7 4.8 %all-to-all-start.1 = ((bf16[8,36,2048]{2,1,0:T(8,128)(2,1)}), bf16[8,36,2048]{2,1,0:T(8,128)(2,1)S(1)}, u32[]{:S(2)}, u32[]{:S(2)}) async-start(bf16[8,36,2048]{2,1,0:T(8,128)(2,1)} %reshape.48), calls=%async_computation.1 | async-start | bytes 2621440 | tf_op jit(solution)/shard_map/all_to_all | solution.py:74
  176.5 4.9 %fusion.42 = f32[288,2048]{1,0:T(8,128)S(1)} fusion(bf16[288,1408]{1,0:T(8,128)(2,1)} %get-tuple-element.10, bf16[2048,1408]{1,0:T(8,128)(2,1)} %constant_dynamic-update-slice_fusion.2), kind=kOutput, calls=%fused_computation.79 | convolution fusion | flops 1660944384 | bytes 8937472 | tf_op jit(solution)/shard_map/dot_general | solution.py:39
  181.4 5.5 %fusion.15 = f32[1024,1408]{1,0:T(8,128)} fusion(bf16[288,1408]{1,0:T(8,128)(2,1)} %get-tuple-element.10, bf16[288,2048]{1,0:T(8,128)(2,1)S(1)} %reshape.47, s32[]{:T(128)S(6)} %select_n.37), kind=kOutput, calls=%fused_computation.36 | convolution fusion | flops 830472192 | bytes 7168004 | tf_op jit(solution)/shard_map/dot_general | solution.py:39
  189.3 4.9 %fusion.4 = bf16[288,2048]{1,0:T(8,128)(2,1)S(1)} fusion(f32[288,2048]{1,0:T(8,128)S(1)} %fusion.42, bf16[288,1408]{1,0:T(8,128)(2,1)} %get-tuple-element.8, bf16[2048,1408]{1,0:T(8,128)(2,1)} %constant_dynamic-update-slice_fusion.4), kind=kOutput, calls=%fused_computation.14 | convolution fusion | flops 1662124032 | bytes 10117120 | tf_op jit(solution)/shard_map/dot_general | solution.py:39
  194.2 4.4 %fusion.19 = f32[704,2048]{1,0:T(8,128)} fusion(bf16[288,2048]{1,0:T(8,128)(2,1)S(1)} %copy-done.8, bf16[288,1408]{1,0:T(8,128)(2,1)S(1)} %copy-done.11, s32[]{:T(128)S(6)} %select_n.41), kind=kOutput, calls=%fused_computation.40 | convolution fusion | flops 830472192 | bytes 7389188 | tf_op jit(solution)/shard_map/dot_general | solution.py:39
  199.8 8.9 %all-to-all-done.1 = bf16[8,36,2048]{2,1,0:T(8,128)(2,1)S(1)} async-done(((bf16[8,36,2048]{2,1,0:T(8,128)(2,1)}), bf16[8,36,2048]{2,1,0:T(8,128)(2,1)S(1)}, u32[]{:S(2)}, u32[]{:S(2)}) %all-to-all-start.1) | async-done | bytes 1179680 | tf_op jit(solution)/shard_map/all_to_all | solution.py:74
  208.7 4.7 %all-to-all-start.3 = ((bf16[8,36,2048]{2,1,0:T(8,128)(2,1)}), bf16[8,36,2048]{2,1,0:T(8,128)(2,1)}, u32[]{:S(2)}, u32[]{:S(2)}) async-start(bf16[8,36,2048]{2,1,0:T(8,128)(2,1)} %reshape.52), calls=%async_computation.3 | async-start | bytes 2621440 | tf_op jit(solution)/shard_map/all_to_all | solution.py:74
  213.4 3.8 %collective-permute-done.9 = bf16[288,704]{1,0:T(8,128)(2,1)} collective-permute-done((bf16[288,704]{1,0:T(8,128)(2,1)S(1)}, bf16[288,704]{1,0:T(8,128)(2,1)}, u32[]{:S(2)}, u32[]{:S(2)}) %collective-permute-start.9) | collective-permute-done | bytes 405536 | tf_op jit(solution)/shard_map/ppermute | solution.py:12
  217.2 6.4 %fusion.2 = bf16[1,704,2048]{2,1,0:T(8,128)(2,1)} fusion(f32[704,2048]{1,0:T(8,128)} %fusion.19, bf16[288,704]{1,0:T(8,128)(2,1)} %collective-permute-done.9, bf16[288,2048]{1,0:T(8,128)(2,1)} %collective-permute-done.10), kind=kOutput, calls=%fused_computation.5 | convolution fusion | flops 833355776 | bytes 10235904 | tf_op jit(solution)/shard_map/dot_general | solution.py:39
  223.7 4.7 %fusion = bf16[1,1024,1408]{2,1,0:T(8,128)(2,1)} fusion(f32[1024,1408]{1,0:T(8,128)S(1)} %bitcast.54, bf16[288,1024]{1,0:T(8,128)(2,1)} %collective-permute-done.6, bf16[288,1408]{1,0:T(8,128)(2,1)} %collective-permute-done.7), kind=kOutput, calls=%fused_computation.3 | convolution fusion | flops 833355776 | bytes 10051584 | tf_op jit(solution)/shard_map/dot_general | solution.py:39
  228.4 6.4 %fusion.1 = bf16[1,1024,1408]{2,1,0:T(8,128)(2,1)} fusion(f32[1024,1408]{1,0:T(8,128)} %fusion.15, bf16[288,1024]{1,0:T(8,128)(2,1)} %collective-permute-done.6, bf16[288,1408]{1,0:T(8,128)(2,1)} %collective-permute-done.8), kind=kOutput, calls=%fused_computation.4 | convolution fusion | flops 833355776 | bytes 10051584 | tf_op jit(solution)/shard_map/dot_general | solution.py:39
  235.6 2.6 %fusion.8 = (f32[128]{0:T(128)S(1)}, f32[128]{0:T(128)S(1)}, bf16[128,2048]{1,0:T(8,128)(2,1)}) fusion(bf16[128,2048]{1,0:T(8,128)(2,1)} %param.10, f32[128,2048]{1,0:T(8,128)S(1)} %fusion.22, f32[128]{0:T(128)S(1)} %get-tuple-element.13, f32[128]{0:T(128)S(1)} %get-tuple-element.12, bf16[288,2048]{1,0:T(8,128)(2,1)S(1)} %reshape.49, ...), kind=kOutput, calls=%fused_computation.30 | convolution fusion | flops 153390848 | bytes 3279360 | tf_op jit(solution)/shard_map/dot_general | solution.py:39
  238.2 7.2 %all-to-all-done.3 = bf16[8,36,2048]{2,1,0:T(8,128)(2,1)} async-done(((bf16[8,36,2048]{2,1,0:T(8,128)(2,1)}), bf16[8,36,2048]{2,1,0:T(8,128)(2,1)}, u32[]{:S(2)}, u32[]{:S(2)}) %all-to-all-start.3) | async-done | bytes 1179680 | tf_op jit(solution)/shard_map/all_to_all | solution.py:74
  (81 shorter events, 44.3 us)
Async XLA Ops:
  0.6 2.1 copy-start
  4.2 8.8 %copy-start.2 = (bf16[1,1024,1408]{2,1,0:T(8,128)(2,1)S(1)}, bf16[1,1024,1408]{2,1,0:T(8,128)(2,1)}, u32[]{:S(2)}) copy-start(bf16[1,1024,1408]{2,1,0:T(8,128)(2,1)} %param.12) | copy-start | bytes 8650756
  6.7 38.6 %all-to-all-start = ((bf16[8,36,2048]{2,1,0:T(8,128)(2,1)}), bf16[8,36,2048]{2,1,0:T(8,128)(2,1)}, u32[]{:S(2)}, u32[]{:S(2)}) async-start(bf16[8,36,2048]{2,1,0:T(8,128)(2,1)} %reshape.46), calls=%async_computation | async-start | bytes 2621440 | tf_op jit(solution)/shard_map/all_to_all | solution.py:74
  13.0 2.7 %copy-start.3 = (bf16[1,1024,1408]{2,1,0:T(8,128)(2,1)S(1)}, bf16[1,1024,1408]{2,1,0:T(8,128)(2,1)}, u32[]{:S(2)}) copy-start(bf16[1,1024,1408]{2,1,0:T(8,128)(2,1)} %param.11) | copy-start | bytes 8650756
  14.2 39.6 %collective-permute-start.2 = (bf16[512,1408]{1,0:T(8,128)(2,1)}, bf16[512,1408]{1,0:T(8,128)(2,1)}, u32[]{:S(2)}, u32[]{:S(2)}) collective-permute-start(bf16[512,1408]{1,0:T(8,128)(2,1)} %dynamic-slice_bitcast_fusion.1), channel_id=1, source_target_pairs={{0,2},{2,0},{1,3},{3,1},{4,6},{6,4},{5,7},{7,5},{8,10},{10,8},{9,1... | collective-permute-start | bytes 4325384 | tf_op jit(solution)/shard_map/ppermute | solution.py:12
  16.9 62.9 %collective-permute-start = (bf16[512,1408]{1,0:T(8,128)(2,1)}, bf16[512,1408]{1,0:T(8,128)(2,1)}, u32[]{:S(2)}, u32[]{:S(2)}) collective-permute-start(bf16[512,1408]{1,0:T(8,128)(2,1)} %dynamic-slice_bitcast_fusion.2), channel_id=1, source_target_pairs={{0,2},{2,0},{1,3},{3,1},{4,6},{6,4},{5,7},{7,5},{8,10},{10,8},{9,1... | collective-permute-start | bytes 4325384 | tf_op jit(solution)/shard_map/ppermute | solution.py:12
  20.6 89.7 %collective-permute-start.4 = (bf16[352,2048]{1,0:T(8,128)(2,1)}, bf16[352,2048]{1,0:T(8,128)(2,1)}, u32[]{:S(2)}, u32[]{:S(2)}) collective-permute-start(bf16[352,2048]{1,0:T(8,128)(2,1)} %dynamic-slice_bitcast_fusion), channel_id=1, source_target_pairs={{0,2},{2,0},{1,3},{3,1},{4,6},{6,4},{5,7},{7,5},{8,10},{10,8},{9,1... | collective-permute-start | bytes 4325384 | tf_op jit(solution)/shard_map/ppermute | solution.py:12
  22.0 0.7 copy-start.12
  22.0 3.2 %copy-start.9 = (bf16[128,2048]{1,0:T(8,128)(2,1)S(1)}, bf16[128,2048]{1,0:T(8,128)(2,1)}, u32[]{:S(2)}) copy-start(bf16[128,2048]{1,0:T(8,128)(2,1)} %param.10) | copy-start | bytes 1572868
  22.7 2.5 %copy-start.6 = (bf16[2048,1408]{1,0:T(8,128)(2,1)}, bf16[2048,1408]{1,0:T(8,128)(2,1)S(1)}, u32[]{:S(2)}) copy-start(bf16[2048,1408]{1,0:T(8,128)(2,1)S(1)} %bitcast_dynamic-update-slice_fusion.1) | copy-start | bytes 17301508
  45.3 78.3 %all-to-all-start.2 = ((bf16[8,36,2048]{2,1,0:T(8,128)(2,1)}), bf16[8,36,2048]{2,1,0:T(8,128)(2,1)S(1)}, u32[]{:S(2)}, u32[]{:S(2)}) async-start(bf16[8,36,2048]{2,1,0:T(8,128)(2,1)} %reshape.50), calls=%async_computation.2 | async-start | bytes 2621440 | tf_op jit(solution)/shard_map/all_to_all | solution.py:74
  49.1 2.9 %copy-start.4 = (bf16[1,1024,1408]{2,1,0:T(8,128)(2,1)S(1)}, bf16[1,1024,1408]{2,1,0:T(8,128)(2,1)}, u32[]{:S(2)}) copy-start(bf16[1,1024,1408]{2,1,0:T(8,128)(2,1)} %param.11) | copy-start | bytes 8650756
  53.8 30.7 %copy-start.5 = (bf16[1,704,2048]{2,1,0:T(8,128)(2,1)S(1)}, bf16[1,704,2048]{2,1,0:T(8,128)(2,1)}, u32[]{:S(2)}) copy-start(bf16[1,704,2048]{2,1,0:T(8,128)(2,1)} %param.13) | copy-start | bytes 8650756
  53.8 71.4 %collective-permute-start.3 = (bf16[512,1408]{1,0:T(8,128)(2,1)}, bf16[512,1408]{1,0:T(8,128)(2,1)}, u32[]{:S(2)}, u32[]{:S(2)}) collective-permute-start(bf16[512,1408]{1,0:T(8,128)(2,1)} %collective-permute-done.2), channel_id=1, source_target_pairs={{0,16},{16,0},{1,17},{17,1},{2,18},{18,2},{3,19},{19,3},{4,20},{20... | collective-permute-start | bytes 4325384 | tf_op jit(solution)/shard_map/ppermute | solution.py:12
  79.8 47.9 %collective-permute-start.1 = (bf16[512,1408]{1,0:T(8,128)(2,1)}, bf16[512,1408]{1,0:T(8,128)(2,1)}, u32[]{:S(2)}, u32[]{:S(2)}) collective-permute-start(bf16[512,1408]{1,0:T(8,128)(2,1)} %collective-permute-done), channel_id=1, source_target_pairs={{0,16},{16,0},{1,17},{17,1},{2,18},{18,2},{3,19},{19,3},{4,20},{20... | collective-permute-start | bytes 4325384 | tf_op jit(solution)/shard_map/ppermute | solution.py:12
  110.3 39.3 %collective-permute-start.5 = (bf16[352,2048]{1,0:T(8,128)(2,1)}, bf16[352,2048]{1,0:T(8,128)(2,1)}, u32[]{:S(2)}, u32[]{:S(2)}) collective-permute-start(bf16[352,2048]{1,0:T(8,128)(2,1)} %collective-permute-done.4), channel_id=1, source_target_pairs={{0,16},{16,0},{1,17},{17,1},{2,18},{18,2},{3,19},{19,3},{4,20},{20... | collective-permute-start | bytes 4325384 | tf_op jit(solution)/shard_map/ppermute | solution.py:12
  122.0 101.7 %collective-permute-start.6 = (bf16[288,1024]{1,0:T(8,128)(2,1)}, bf16[288,1024]{1,0:T(8,128)(2,1)}, u32[]{:S(2)}, u32[]{:S(2)}) collective-permute-start(bf16[288,1024]{1,0:T(8,128)(2,1)} %constant_dynamic-slice_fusion.1), channel_id=1, source_target_pairs={{0,2},{2,0},{1,3},{3,1},{4,6},{6,4},{5,7},{7,5},{8,10},{10,8},{9,1... | collective-permute-start | bytes 1769480 | tf_op jit(solution)/shard_map/ppermute | solution.py:12
  124.7 88.6 %collective-permute-start.10 = (bf16[288,2048]{1,0:T(8,128)(2,1)}, bf16[288,2048]{1,0:T(8,128)(2,1)}, u32[]{:S(2)}, u32[]{:S(2)}) collective-permute-start(bf16[288,2048]{1,0:T(8,128)(2,1)} %reshape.51), channel_id=1, source_target_pairs={{0,2},{2,0},{1,3},{3,1},{4,6},{6,4},{5,7},{7,5},{8,10},{10,8},{9,1... | collective-permute-start | bytes 3538952 | tf_op jit(solution)/shard_map/ppermute | solution.py:12
  139.6 12.7 %copy-start.7 = (bf16[288,2048]{1,0:T(8,128)(2,1)S(1)}, bf16[288,2048]{1,0:T(8,128)(2,1)}, u32[]{:S(2)}) copy-start(bf16[288,2048]{1,0:T(8,128)(2,1)} %reshape.51) | copy-start | bytes 3538948
  158.7 7.1 %copy-start.10 = (bf16[288,1408]{1,0:T(8,128)(2,1)}, bf16[288,1408]{1,0:T(8,128)(2,1)S(1)}, u32[]{:S(2)}) copy-start(bf16[288,1408]{1,0:T(8,128)(2,1)S(1)} %get-tuple-element.9) | copy-start | bytes 2433028
  164.4 59.3 %collective-permute-start.7 = (bf16[288,1408]{1,0:T(8,128)(2,1)}, bf16[288,1408]{1,0:T(8,128)(2,1)}, u32[]{:S(2)}, u32[]{:S(2)}) collective-permute-start(bf16[288,1408]{1,0:T(8,128)(2,1)} %get-tuple-element.8), channel_id=1, source_target_pairs={{0,2},{2,0},{1,3},{3,1},{4,6},{6,4},{5,7},{7,5},{8,10},{10,8},{9,1... | collective-permute-start | bytes 2433032 | tf_op jit(solution)/shard_map/ppermute | solution.py:12
  171.7 37.0 %all-to-all-start.1 = ((bf16[8,36,2048]{2,1,0:T(8,128)(2,1)}), bf16[8,36,2048]{2,1,0:T(8,128)(2,1)S(1)}, u32[]{:S(2)}, u32[]{:S(2)}) async-start(bf16[8,36,2048]{2,1,0:T(8,128)(2,1)} %reshape.48), calls=%async_computation.1 | async-start | bytes 2621440 | tf_op jit(solution)/shard_map/all_to_all | solution.py:74
  181.4 6.2 %copy-start.11 = (bf16[288,1408]{1,0:T(8,128)(2,1)S(1)}, bf16[288,1408]{1,0:T(8,128)(2,1)}, u32[]{:S(2)}) copy-start(bf16[288,1408]{1,0:T(8,128)(2,1)} %copy-done.10) | copy-start | bytes 2433028
  187.0 41.4 %collective-permute-start.8 = (bf16[288,1408]{1,0:T(8,128)(2,1)}, bf16[288,1408]{1,0:T(8,128)(2,1)}, u32[]{:S(2)}, u32[]{:S(2)}) collective-permute-start(bf16[288,1408]{1,0:T(8,128)(2,1)} %get-tuple-element.10), channel_id=1, source_target_pairs={{0,2},{2,0},{1,3},{3,1},{4,6},{6,4},{5,7},{7,5},{8,10},{10,8},{9,1... | collective-permute-start | bytes 2433032 | tf_op jit(solution)/shard_map/ppermute | solution.py:12
  187.8 6.4 %copy-start.8 = (bf16[288,2048]{1,0:T(8,128)(2,1)S(1)}, bf16[288,2048]{1,0:T(8,128)(2,1)}, u32[]{:S(2)}) copy-start(bf16[288,2048]{1,0:T(8,128)(2,1)} %reshape.51) | copy-start | bytes 3538948
  187.8 29.4 %collective-permute-start.9 = (bf16[288,704]{1,0:T(8,128)(2,1)S(1)}, bf16[288,704]{1,0:T(8,128)(2,1)}, u32[]{:S(2)}, u32[]{:S(2)}) collective-permute-start(bf16[288,704]{1,0:T(8,128)(2,1)S(1)} %constant_dynamic-slice_fusion), channel_id=1, source_target_pairs={{0,2},{2,0},{1,3},{3,1},{4,6},{6,4},{5,7},{7,5},{8,10},{10,8},{9,1... | collective-permute-start | bytes 1216520 | tf_op jit(solution)/shard_map/ppermute | solution.py:12
  208.7 15.0 %slice-start = ((s8[5767168]{0:T(1024)(128)(4,1)}), s8[1572864]{0:T(1024)(128)(4,1)S(1)}, s32[]{:S(2)}) async-start(s8[5767168]{0:T(1024)(128)(4,1)} %bitcast.53), calls=%async_computation.4 | async-start | bytes 3145728
  208.7 36.6 %all-to-all-start.3 = ((bf16[8,36,2048]{2,1,0:T(8,128)(2,1)}), bf16[8,36,2048]{2,1,0:T(8,128)(2,1)}, u32[]{:S(2)}, u32[]{:S(2)}) async-start(bf16[8,36,2048]{2,1,0:T(8,128)(2,1)} %reshape.52), calls=%async_computation.3 | async-start | bytes 2621440 | tf_op jit(solution)/shard_map/all_to_all | solution.py:74
  213.4 10.3 %slice-start.1 = ((s8[5767168]{0:T(1024)(128)(4,1)}), s8[4194304]{0:T(1024)(128)(4,1)S(1)}, s32[]{:S(2)}) async-start(s8[5767168]{0:T(1024)(128)(4,1)} %bitcast.53), calls=%async_computation.5 | async-start | bytes 8388608
  235.6 13.0 %copy-start.1 = (bf16[128,2048]{1,0:T(8,128)(2,1)S(1)}, bf16[128,2048]{1,0:T(8,128)(2,1)}, u32[]{:S(2)}) copy-start(bf16[128,2048]{1,0:T(8,128)(2,1)} %param.7) | copy-start | bytes 1572868

commit v2 on v1

--- a/solution.py
+++ b/solution.py
@@ -12,26 +12,43 @@
     return lax.ppermute(value, axis, [(i, (i + step) % size) for i in range(size)])
 
 
-def gather_weight(weight):
-    rows, cols = weight.shape
-    n_replica = lax.axis_size("dp")
+def pieces_of(weight):
+    rows = weight.shape[0]
     n_group = lax.axis_size("groups")
-    me = lax.axis_index("dp")
     group = lax.axis_index("groups")
     if rows % (16 * n_group):
         n_group, group = 1, 0
     share = rows // n_group
-    mine = lax.dynamic_slice_in_dim(weight, group * share, share, 0)
+    chunks = 2 if share % 32 == 0 else 1
+    size = share // chunks
+    return [
+        lax.dynamic_slice_in_dim(weight, group * share + c * size, size, 0) for c in range(chunks)
+    ]
+
+
+def fetch(mine):
+    return [[shift(chunk, "dp", step) for chunk in mine] for step in range(1, lax.axis_size("dp"))]
+
+
+def gather_weight(weight, fetched):
+    rows, cols = weight.shape
+    n_replica = lax.axis_size("dp")
+    me = lax.axis_index("dp")
+    size = fetched[0][0].shape[0]
+    share = size * len(fetched[0])
+    n_group = rows // share
+    group = lax.axis_index("groups") if n_group > 1 else 0
     full = jnp.zeros((n_replica * rows, cols), weight.dtype)
     full = lax.dynamic_update_slice_in_dim(full, weight, me * rows, 0)
     for step in range(1, n_replica):
         owner = lax.rem(me - step + n_replica, n_replica)
-        piece = shift(mine, "dp", step)
-        full = lax.dynamic_update_slice_in_dim(full, piece, owner * rows + group * share, 0)
-        for hop in range(1, n_group):
-            other = shift(piece, "groups", hop)
-            origin = lax.rem(group - hop + n_group, n_group)
-            full = lax.dynamic_update_slice_in_dim(full, other, owner * rows + origin * share, 0)
+        for c, piece in enumerate(fetched[step - 1]):
+            base = owner * rows + c * size
+            full = lax.dynamic_update_slice_in_dim(full, piece, base + group * share, 0)
+            for hop in range(1, n_group):
+                other = shift(piece, "groups", hop)
+                origin = lax.rem(group - hop + n_group, n_group)
+                full = lax.dynamic_update_slice_in_dim(full, other, base + origin * share, 0)
     return full
 
 
@@ -51,9 +68,9 @@
     row_count = tok_rows * chosen
     slots = experts * capacity
 
-    full_gate = gather_weight(w_gate[0])
-    full_up = gather_weight(w_up[0])
-    full_down = gather_weight(w_down[0])
+    gate_mine, up_mine, down_mine = (pieces_of(w[0]) for w in (w_gate, w_up, w_down))
+    gate_mine, expert_ids = lax.optimization_barrier((gate_mine, expert_ids))
+    gate_fetched, up_fetched = fetch(gate_mine), fetch(up_mine)
 
     flat_ids = expert_ids.reshape(row_count)
     order = jnp.arange(row_count, dtype=jnp.int32)
@@ -74,38 +91,49 @@
         value = lax.all_to_all(value, ("expert", "pair"), split_axis=0, concat_axis=0, tiled=True)
         return value.reshape(slots, model_width)
 
+    def part(value, index):
+        width = value.shape[1] // n_replica
+        return lax.dynamic_slice_in_dim(value, index * width, width, 1)
+
+    def to_replicas(value, split=False):
+        targets = [lax.rem(me + step, n_replica) for step in range(n_replica)]
+        sent = [part(value, target) if split else value for target in targets]
+        return sent[:1] + [shift(sent[step], "dp", step) for step in range(1, n_replica)]
+
     rows = exchange(send_rows)
+    rows, send_grads, down_mine, gate_fetched[0][-1] = lax.optimization_barrier(
+        (rows, send_grads, down_mine, gate_fetched[0][-1])
+    )
     grads = exchange(send_grads)
+    down_fetched = fetch(down_mine)
+    full_gate = gather_weight(w_gate[0], gate_fetched)
+    full_up = gather_weight(w_up[0], up_fetched)
+    full_down = gather_weight(w_down[0], down_fetched)
+    all_rows = to_replicas(rows, split=True)
+    all_grads = to_replicas(grads)
     gate_pre = dot(rows, full_gate)
     up_pre = dot(rows, full_up)
     squash = jax.nn.sigmoid(gate_pre)
     active = gate_pre * squash
-    hidden = (active * up_pre).astype(BF16)
+    hidden, full_down = lax.optimization_barrier(((active * up_pre).astype(BF16), full_down))
     output = dot(hidden, full_down).astype(BF16)
     back_out = exchange(output)
-    hidden_grad = dot(grads, full_down, 1, 1)
+    all_rows, held_grads = lax.optimization_barrier((all_rows, grads))
+    hidden_grad = dot(held_grads, full_down, 1, 1)
     gate_grad = (hidden_grad * up_pre * (squash + active * (1.0 - squash))).astype(BF16)
     up_grad = (hidden_grad * active).astype(BF16)
-    input_grad = (dot(gate_grad, full_gate, 1, 1) + dot(up_grad, full_up, 1, 1)).astype(BF16)
+    all_gate = to_replicas(gate_grad)
+    all_up = to_replicas(up_grad)
+    all_hidden = to_replicas(hidden, split=True)
+    all_grads, held_gate = lax.optimization_barrier((all_grads, gate_grad))
+    input_grad = (dot(held_gate, full_gate, 1, 1) + dot(up_grad, full_up, 1, 1)).astype(BF16)
     back_grad = exchange(input_grad)
 
-    def part(value, index):
-        width = value.shape[1] // n_replica
-        return lax.dynamic_slice_in_dim(value, index * width, width, 1)
-
-    sum_gate = dot(part(rows, me), gate_grad, 0, 0)
-    sum_up = dot(part(rows, me), up_grad, 0, 0)
-    sum_down = dot(part(hidden, me), grads, 0, 0)
-    for step in range(1, n_replica):
-        target = lax.rem(me + step, n_replica)
-        their_grads = shift(grads, "dp", step)
-        their_rows = shift(part(rows, target), "dp", step)
-        their_hidden = shift(part(hidden, target), "dp", step)
-        their_gate = shift(gate_grad, "dp", step)
-        their_up = shift(up_grad, "dp", step)
-        sum_down += dot(their_hidden, their_grads, 0, 0)
-        sum_gate += dot(their_rows, their_gate, 0, 0)
-        sum_up += dot(their_rows, their_up, 0, 0)
+    joined = [jnp.concatenate(v, 0) for v in (all_rows, all_hidden, all_gate, all_up, all_grads)]
+    all_rows, all_hidden, all_gate, all_up, all_grads = joined
+    sum_gate = dot(all_rows, all_gate, 0, 0)
+    sum_up = dot(all_rows, all_up, 0, 0)
+    sum_down = dot(all_hidden, all_grads, 0, 0)
 
     out_rows = [dot(picks[k], back_out, 0, 0) for k in range(chosen)]
     result = sum(gate_weights[:, k : k + 1] * out_rows[k] for k in range(chosen)).astype(BF16)

time: 250 us -> 236 us (0.944)
  matrix products: 70.2 us -> 55.5 us
  waiting for transfers between devices: 96.3 us -> 83 us
  local copies, waits for them, and re-layouts: 46.6 us -> 54.2 us
  starting transfers between devices: 33.1 us -> 40.1 us
    all_to_all x4, waiting for transfers between devices: 33.9 us -> 3.07 us  [exchange(): lax.all_to_all(value, ('expert', 'pair'), split_axis=0, concat_axis=0, ti...]
    ppermute x11 -> x17, waiting for transfers between devices: 62.4 us -> 79.9 us  [shift(): lax.ppermute(value, axis, [(i, (i + step) % size) for i in range(size)])]
    dot_general x18 -> x15, matrix products: 70.2 us -> 55.5 us  [dot(): lax.dot_general(a, b, (((a_dim,), (b_dim,)), ((), ())), preferred_element...]
    ppermute x11 -> x17, starting transfers between devices: 13.6 us -> 19.8 us  [shift(): lax.ppermute(value, axis, [(i, (i + step) % size) for i in range(size)])]
    dynamic_update_slice x6 -> x12, local copies, waits for them, and re-layouts: 15.6 us -> 20 us  [the longest x6 12.2 us: gather_weight(): full = lax.dynamic_update_slice_in_dim(full, piece, base + group * share, 0)]
  transfers between devices with their start and end apart: 15 -> 21, of which waited for: 7 -> 10; matrix products, arithmetic and copies ran while one was open for 43% -> 42% of each run, Pallas kernels for 0% -> 0%
where the time goes in v2:
time: 236 us; the launch traced here: 235 us
  waiting for transfers between devices  83 us (35%)
  matrix products  55.5 us (24%)
  local copies, waits for them, and re-layouts  54.2 us (23%)
  starting transfers between devices  40.1 us (17%)
    ppermute x17, waiting for transfers between devices, shift(): lax.ppermute(value, axis, [(i, (i + step) % size) for i in range(size)])  79.9 us
    dot_general x15, matrix products, dot(): lax.dot_general(a, b, (((a_dim,), (b_dim,)), ((), ())), preferred_element...  55.5 us
    all_to_all x4, starting transfers between devices, exchange(): lax.all_to_all(value, ('expert', 'pair'), split_axis=0, concat_axis=0, ti...  20.3 us
    ppermute x17, starting transfers between devices, shift(): lax.ppermute(value, axis, [(i, (i + step) % size) for i in range(size)])  19.8 us
    dynamic_update_slice x6, local copies, waits for them, and re-layouts, gather_weight(): full = lax.dynamic_update_slice_in_dim(full, piece, base + group * share, 0)  12.2 us
    dynamic_update_slice x6, local copies, waits for them, and re-layouts, gather_weight(): lax.dynamic_update_slice_in_dim(full, other, base + origin * share, 0)  7.74 us
    reshape x4, local copies, waits for them, and re-layouts, exchange(): value = value.reshape(experts, capacity, model_width)  7.05 us
    dynamic_slice x3, local copies, waits for them, and re-layouts, pieces_of(): lax.dynamic_slice_in_dim(weight, group * share + c * size, size, 0)  5.07 us
  transfers between devices with their start and end apart: 21, of which 10 were waited for; matrix products, arithmetic and copies ran while one was open for 42% of the time, Pallas kernels for 0%

profile of v2, /device:TPU:0, one launch (start us, length us, event | category | flops | bytes accessed | tf_op | source)
XLA Modules:
  0.0 234.5 jit_solution(15117393020087739873)
XLA Ops:
  0.7 2.6 %dynamic-slice_bitcast_fusion.4 = (bf16[256,1408]{1,0:T(8,128)(2,1)}, bf16[256,1408]{1,0:T(8,128)(2,1)}) fusion(bf16[1,1024,1408]{2,1,0:T(8,128)(2,1)} %param.11, s32[]{:T(128)S(6)} %select_n.62, s32[]{:T(128)S(6)} %select_n.61), kind=kLoop, calls=%fused_computation.46 | loop fusion | bytes 2883592 | tf_op jit(solution)/shard_map/dynamic_slice | solution.py:25
  5.4 2.4 %reshape.49 = bf16[8,36,2048]{2,1,0:T(8,128)(2,1)} reshape(bf16[288,2048]{1,0:T(8,128)(2,1)} %convolution_convert_fusion.3) | data formatting | bytes 2359296 | tf_op jit(solution)/shard_map/reshape | solution.py:90
  7.8 6.3 %all-to-all-start = ((bf16[8,36,2048]{2,1,0:T(8,128)(2,1)}), bf16[8,36,2048]{2,1,0:T(8,128)(2,1)}, u32[]{:S(2)}, u32[]{:S(2)}) async-start(bf16[8,36,2048]{2,1,0:T(8,128)(2,1)} %reshape.49), calls=%async_computation | async-start | bytes 2621440 | tf_op jit(solution)/shard_map/all_to_all | solution.py:91
  21.7 3.1 %broadcast.11.clone.1 = bf16[2048,1408]{1,0:T(8,128)(2,1)} broadcast(bf16[]{:T(256)} %constant.54.clone.1), dimensions={} | broadcast | bytes 5767170 | tf_op jit(solution)/shard_map/broadcast.3
  27.9 3.2 %broadcast_in_dim.16 = bf16[1408,2048]{1,0:T(8,128)(2,1)} broadcast(bf16[]{:T(256)} %constant.54.clone.1), dimensions={} | broadcast | bytes 5767170 | tf_op jit(solution)/shard_map/broadcast_in_dim | solution.py:41
  35.0 13.8 %collective-permute-done.1 = bf16[256,1408]{1,0:T(8,128)(2,1)} collective-permute-done((bf16[256,1408]{1,0:T(8,128)(2,1)}, bf16[256,1408]{1,0:T(8,128)(2,1)}, u32[]{:S(2)}, u32[]{:S(2)}) %collective-permute-start.1) | collective-permute-done | bytes 720928 | tf_op jit(solution)/shard_map/ppermute | solution.py:12
  51.6 12.7 %collective-permute-done.4 = bf16[256,1408]{1,0:T(8,128)(2,1)} collective-permute-done((bf16[256,1408]{1,0:T(8,128)(2,1)}, bf16[256,1408]{1,0:T(8,128)(2,1)}, u32[]{:S(2)}, u32[]{:S(2)}) %collective-permute-start.4) | collective-permute-done | bytes 720928 | tf_op jit(solution)/shard_map/ppermute | solution.py:12
  65.8 13.5 %collective-permute-done.6 = bf16[256,1408]{1,0:T(8,128)(2,1)} collective-permute-done((bf16[256,1408]{1,0:T(8,128)(2,1)}, bf16[256,1408]{1,0:T(8,128)(2,1)}, u32[]{:S(2)}, u32[]{:S(2)}) %collective-permute-start.6) | collective-permute-done | bytes 720928 | tf_op jit(solution)/shard_map/ppermute | solution.py:12
  90.9 2.0 constant_dynamic-update-slice_fusion.5
  92.9 5.8 %collective-permute-done.7 = bf16[256,1408]{1,0:T(8,128)(2,1)} collective-permute-done((bf16[256,1408]{1,0:T(8,128)(2,1)}, bf16[256,1408]{1,0:T(8,128)(2,1)}, u32[]{:S(2)}, u32[]{:S(2)}) %collective-permute-start.7) | collective-permute-done | bytes 720928 | tf_op jit(solution)/shard_map/ppermute | solution.py:12
  98.7 2.0 constant_dynamic-update-slice_fusion.4
  101.9 4.8 %all-to-all-start.2 = ((bf16[8,36,2048]{2,1,0:T(8,128)(2,1)}), bf16[8,36,2048]{2,1,0:T(8,128)(2,1)S(1)}, u32[]{:S(2)}, u32[]{:S(2)}) async-start(bf16[8,36,2048]{2,1,0:T(8,128)(2,1)} %reshape.53), calls=%async_computation.2 | async-start | bytes 2621440 | tf_op jit(solution)/shard_map/all_to_all | solution.py:91
  112.8 10.9 %collective-permute-done.10 = bf16[176,2048]{1,0:T(8,128)(2,1)} collective-permute-done((bf16[176,2048]{1,0:T(8,128)(2,1)}, bf16[176,2048]{1,0:T(8,128)(2,1)}, u32[]{:S(2)}, u32[]{:S(2)}) %collective-permute-start.10) | collective-permute-done | bytes 720928 | tf_op jit(solution)/shard_map/ppermute | solution.py:12
  127.2 4.6 %fusion.46 = f32[288,1408]{1,0:T(8,128)S(1)} fusion(bf16[288,2048]{1,0:T(8,128)(2,1)S(1)} %reshape.50, bf16[2048,1408]{1,0:T(8,128)(2,1)} %constant_dynamic-update-slice_fusion.8), kind=kOutput, calls=%fused_computation.96 | convolution fusion | flops 1660944384 | bytes 8568832 | tf_op jit(solution)/shard_map/dot_general | solution.py:56
  131.9 6.7 %multiply_convert_fusion.2 = (bf16[288,1408]{1,0:T(8,128)(2,1)}, f32[288,1408]{1,0:T(8,128)}) fusion(f32[288,1408]{1,0:T(8,128)S(1)} %fusion.46, bf16[288,2048]{1,0:T(8,128)(2,1)S(1)} %reshape.50, bf16[2048,1408]{1,0:T(8,128)(2,1)} %constant_dynamic-update-slice_fusion.4), kind=kOutput, calls=%fused_computation.31 | convolution fusion | flops 1663377408 | bytes 11001856 | tf_op jit(solution)/shard_map/dot_general | solution.py:56
  138.6 2.1 constant_dynamic-update-slice_fusion.3
  141.6 2.1 constant_dynamic-update-slice_fusion.1
  147.1 4.9 %convolution_convert_fusion.4 = bf16[288,2048]{1,0:T(8,128)(2,1)S(1)} fusion(bf16[288,1408]{1,0:T(8,128)(2,1)} %get-tuple-element.29, bf16[1408,2048]{1,0:T(8,128)(2,1)} %constant_dynamic-update-slice_fusion), kind=kOutput, calls=%fused_computation.13 | convolution fusion | flops 1661534208 | bytes 7757824 | tf_op jit(solution)/shard_map/dot_general | solution.py:56
  153.1 4.7 %all-to-all-start.1 = ((bf16[8,36,2048]{2,1,0:T(8,128)(2,1)}), bf16[8,36,2048]{2,1,0:T(8,128)(2,1)S(1)}, u32[]{:S(2)}, u32[]{:S(2)}) async-start(bf16[8,36,2048]{2,1,0:T(8,128)(2,1)} %reshape.51), calls=%async_computation.1 | async-start | bytes 2621440 | tf_op jit(solution)/shard_map/all_to_all | solution.py:91
  157.9 2.5 %constant_dynamic-slice_fusion.1 = (bf16[288,704]{1,0:T(8,128)(2,1)S(1)}, bf16[288,704]{1,0:T(8,128)(2,1)}) fusion(bf16[288,1408]{1,0:T(8,128)(2,1)} %get-tuple-element.29, s32[]{:T(128)S(6)} %select_n.77, s32[]{:T(128)S(6)} %select_n.78), kind=kLoop, calls=%fused_computation.70 | loop fusion | bytes 1622024 | tf_op jit(solution)/shard_map/dynamic_slice | solution.py:96
  161.9 7.2 %multiply_convert_fusion = (bf16[288,1408]{1,0:T(8,128)(2,1)}, bf16[288,1408]{1,0:T(8,128)(2,1)}) fusion(f32[288,1408]{1,0:T(8,128)} %copy-done.14, f32[288,1408]{1,0:T(8,128)} %get-tuple-element.58, bf16[288,2048]{1,0:T(8,128)(2,1)S(1)} %reshape.54, bf16[1408,2048]{1,0:T(8,128)(2,1)} %constant_dynamic-update-slice_fusion), kind=kOutput, calls=%fused_computation.29 | convolution fusion | flops 1665810432 | bytes 11812864 | tf_op jit(solution)/shard_map/dot_general | solution.py:56
  171.1 4.5 %collective-permute-done.12 = bf16[288,2048]{1,0:T(8,128)(2,1)} collective-permute-done((bf16[288,2048]{1,0:T(8,128)(2,1)S(1)}, bf16[288,2048]{1,0:T(8,128)(2,1)}, u32[]{:S(2)}, u32[]{:S(2)}) %collective-permute-start.12) | collective-permute-done | bytes 1179680 | tf_op jit(solution)/shard_map/ppermute | solution.py:12
  175.6 3.2 %fusion.47 = f32[288,2048]{1,0:T(8,128)S(1)} fusion(bf16[288,1408]{1,0:T(8,128)(2,1)} %get-tuple-element.33, bf16[2048,1408]{1,0:T(8,128)(2,1)S(1)} %bitcast.53), kind=kOutput, calls=%fused_computation.97 | convolution fusion | flops 1660944384 | bytes 8937472 | tf_op jit(solution)/shard_map/dot_general | solution.py:56
  178.8 6.0 %fusion.4 = bf16[288,2048]{1,0:T(8,128)(2,1)} fusion(f32[288,2048]{1,0:T(8,128)S(1)} %fusion.47, bf16[288,1408]{1,0:T(8,128)(2,1)} %get-tuple-element.40, bf16[2048,1408]{1,0:T(8,128)(2,1)} %constant_dynamic-update-slice_fusion.4), kind=kOutput, calls=%fused_computation.14 | convolution fusion | flops 1662124032 | bytes 10117120 | tf_op jit(solution)/shard_map/dot_general | solution.py:56
  184.7 2.3 reshape.55
  187.0 3.1 %all-to-all-done.1 = bf16[8,36,2048]{2,1,0:T(8,128)(2,1)S(1)} async-done(((bf16[8,36,2048]{2,1,0:T(8,128)(2,1)}), bf16[8,36,2048]{2,1,0:T(8,128)(2,1)S(1)}, u32[]{:S(2)}, u32[]{:S(2)}) %all-to-all-start.1) | async-done | bytes 1179680 | tf_op jit(solution)/shard_map/all_to_all | solution.py:91
  190.1 4.5 %all-to-all-start.3 = ((bf16[8,36,2048]{2,1,0:T(8,128)(2,1)}), bf16[8,36,2048]{2,1,0:T(8,128)(2,1)}, u32[]{:S(2)}, u32[]{:S(2)}) async-start(bf16[8,36,2048]{2,1,0:T(8,128)(2,1)} %reshape.55), calls=%async_computation.3 | async-start | bytes 2621440 | tf_op jit(solution)/shard_map/all_to_all | solution.py:91
  195.8 6.7 %collective-permute-done.14 = bf16[288,1408]{1,0:T(8,128)(2,1)} collective-permute-done((bf16[288,1408]{1,0:T(8,128)(2,1)}, bf16[288,1408]{1,0:T(8,128)(2,1)}, u32[]{:S(2)}, u32[]{:S(2)}) %collective-permute-start.14) | collective-permute-done | bytes 811040 | tf_op jit(solution)/shard_map/ppermute | solution.py:12
  202.4 5.3 %fusion = bf16[1,1024,1408]{2,1,0:T(8,128)(2,1)} fusion(bf16[576,1024]{1,0:T(8,128)(2,1)S(1)} %constant_dynamic-update-slice_fusion.12, bf16[288,1408]{1,0:T(8,128)(2,1)} %collective-permute-done.14, bf16[288,1408]{1,0:T(8,128)(2,1)} %get-tuple-element.33), kind=kOutput, calls=%fused_computation.3 | convolution fusion | flops 1665630208 | bytes 5685248 | tf_op jit(solution)/shard_map/dot_general | solution.py:56
  207.8 10.4 %collective-permute-done.15 = bf16[288,1408]{1,0:T(8,128)(2,1)} collective-permute-done((bf16[288,1408]{1,0:T(8,128)(2,1)}, bf16[288,1408]{1,0:T(8,128)(2,1)}, u32[]{:S(2)}, u32[]{:S(2)}) %collective-permute-start.15) | collective-permute-done | bytes 811040 | tf_op jit(solution)/shard_map/ppermute | solution.py:12
  218.2 5.3 %fusion.1 = bf16[1,1024,1408]{2,1,0:T(8,128)(2,1)} fusion(bf16[576,1024]{1,0:T(8,128)(2,1)S(1)} %constant_dynamic-update-slice_fusion.12, bf16[288,1408]{1,0:T(8,128)(2,1)} %collective-permute-done.15, bf16[288,1408]{1,0:T(8,128)(2,1)} %get-tuple-element.40), kind=kOutput, calls=%fused_computation.4 | convolution fusion | flops 1665630208 | bytes 5685248 | tf_op jit(solution)/shard_map/dot_general | solution.py:56
  223.5 5.4 %fusion.2 = bf16[1,704,2048]{2,1,0:T(8,128)(2,1)} fusion(bf16[288,2048]{1,0:T(8,128)(2,1)} %collective-permute-done.12, bf16[288,2048]{1,0:T(8,128)(2,1)S(1)} %copy-done.11, bf16[288,704]{1,0:T(8,128)(2,1)} %collective-permute-done.16, bf16[288,704]{1,0:T(8,128)(2,1)S(1)} %get-tuple-element.51), kind=kOutput, calls=%fused_computation.5 | convolution fusion | flops 1668726784 | bytes 6053888 | tf_op jit(solution)/shard_map/dot_general | solution.py:56
  (102 shorter events, 59.0 us)
Async XLA Ops:
  5.4 10.7 %copy-start.3 = (bf16[1,1024,1408]{2,1,0:T(8,128)(2,1)S(1)}, bf16[1,1024,1408]{2,1,0:T(8,128)(2,1)}, u32[]{:S(2)}) copy-start(bf16[1,1024,1408]{2,1,0:T(8,128)(2,1)} %param.12) | copy-start | bytes 8650756
  7.8 79.0 %all-to-all-start = ((bf16[8,36,2048]{2,1,0:T(8,128)(2,1)}), bf16[8,36,2048]{2,1,0:T(8,128)(2,1)}, u32[]{:S(2)}, u32[]{:S(2)}) async-start(bf16[8,36,2048]{2,1,0:T(8,128)(2,1)} %reshape.49), calls=%async_computation | async-start | bytes 2621440 | tf_op jit(solution)/shard_map/all_to_all | solution.py:91
  14.1 74.2 %collective-permute-start = (bf16[256,1408]{1,0:T(8,128)(2,1)}, bf16[256,1408]{1,0:T(8,128)(2,1)}, u32[]{:S(2)}, u32[]{:S(2)}) collective-permute-start(bf16[256,1408]{1,0:T(8,128)(2,1)} %get-tuple-element.23), channel_id=1, source_target_pairs={{0,2},{2,0},{1,3},{3,1},{4,6},{6,4},{5,7},{7,5},{8,10},{10,8},{9,1... | collective-permute-start | bytes 2162696 | tf_op jit(solution)/shard_map/ppermute | solution.py:12
  15.6 33.2 %collective-permute-start.1 = (bf16[256,1408]{1,0:T(8,128)(2,1)}, bf16[256,1408]{1,0:T(8,128)(2,1)}, u32[]{:S(2)}, u32[]{:S(2)}) collective-permute-start(bf16[256,1408]{1,0:T(8,128)(2,1)} %get-tuple-element.25), channel_id=1, source_target_pairs={{0,2},{2,0},{1,3},{3,1},{4,6},{6,4},{5,7},{7,5},{8,10},{10,8},{9,1... | collective-permute-start | bytes 2162696 | tf_op jit(solution)/shard_map/ppermute | solution.py:12
  17.4 46.9 %collective-permute-start.4 = (bf16[256,1408]{1,0:T(8,128)(2,1)}, bf16[256,1408]{1,0:T(8,128)(2,1)}, u32[]{:S(2)}, u32[]{:S(2)}) collective-permute-start(bf16[256,1408]{1,0:T(8,128)(2,1)} %get-tuple-element.43), channel_id=1, source_target_pairs={{0,2},{2,0},{1,3},{3,1},{4,6},{6,4},{5,7},{7,5},{8,10},{10,8},{9,1... | collective-permute-start | bytes 2162696 | tf_op jit(solution)/shard_map/ppermute | solution.py:12
  18.9 60.5 %collective-permute-start.6 = (bf16[256,1408]{1,0:T(8,128)(2,1)}, bf16[256,1408]{1,0:T(8,128)(2,1)}, u32[]{:S(2)}, u32[]{:S(2)}) collective-permute-start(bf16[256,1408]{1,0:T(8,128)(2,1)} %get-tuple-element.42), channel_id=1, source_target_pairs={{0,2},{2,0},{1,3},{3,1},{4,6},{6,4},{5,7},{7,5},{8,10},{10,8},{9,1... | collective-permute-start | bytes 2162696 | tf_op jit(solution)/shard_map/ppermute | solution.py:12
  21.7 4.4 %copy-start.6 = (bf16[2048,1408]{1,0:T(8,128)(2,1)}, bf16[2048,1408]{1,0:T(8,128)(2,1)S(1)}, u32[]{:S(2)}) copy-start(bf16[2048,1408]{1,0:T(8,128)(2,1)S(1)} %bitcast_dynamic-update-slice_fusion.2) | copy-start | bytes 17301508
  33.5 16.9 %copy-start.5 = (bf16[1,704,2048]{2,1,0:T(8,128)(2,1)S(1)}, bf16[1,704,2048]{2,1,0:T(8,128)(2,1)}, u32[]{:S(2)}) copy-start(bf16[1,704,2048]{2,1,0:T(8,128)(2,1)} %param.13) | copy-start | bytes 8650756
  48.8 36.1 %collective-permute-start.2 = (bf16[256,1408]{1,0:T(8,128)(2,1)}, bf16[256,1408]{1,0:T(8,128)(2,1)S(1)}, u32[]{:S(2)}, u32[]{:S(2)}) collective-permute-start(bf16[256,1408]{1,0:T(8,128)(2,1)} %collective-permute-done.1), channel_id=1, source_target_pairs={{0,16},{16,0},{1,17},{17,1},{2,18},{18,2},{3,19},{19,3},{4,20},{20... | collective-permute-start | bytes 2162696 | tf_op jit(solution)/shard_map/ppermute | solution.py:12
  64.3 21.6 %collective-permute-start.5 = (bf16[256,1408]{1,0:T(8,128)(2,1)}, bf16[256,1408]{1,0:T(8,128)(2,1)S(1)}, u32[]{:S(2)}, u32[]{:S(2)}) collective-permute-start(bf16[256,1408]{1,0:T(8,128)(2,1)} %collective-permute-done.4), channel_id=1, source_target_pairs={{0,16},{16,0},{1,17},{17,1},{2,18},{18,2},{3,19},{19,3},{4,20},{20... | collective-permute-start | bytes 2162696 | tf_op jit(solution)/shard_map/ppermute | solution.py:12
  79.3 19.4 %collective-permute-start.7 = (bf16[256,1408]{1,0:T(8,128)(2,1)}, bf16[256,1408]{1,0:T(8,128)(2,1)}, u32[]{:S(2)}, u32[]{:S(2)}) collective-permute-start(bf16[256,1408]{1,0:T(8,128)(2,1)} %collective-permute-done.6), channel_id=1, source_target_pairs={{0,16},{16,0},{1,17},{17,1},{2,18},{18,2},{3,19},{19,3},{4,20},{20... | collective-permute-start | bytes 2162696 | tf_op jit(solution)/shard_map/ppermute | solution.py:12
  86.8 14.0 %copy-start.7 = (bf16[288,2048]{1,0:T(8,128)(2,1)S(1)}, bf16[288,2048]{1,0:T(8,128)(2,1)}, u32[]{:S(2)}) copy-start(bf16[288,2048]{1,0:T(8,128)(2,1)} %fusion.3) | copy-start | bytes 3538948
  88.3 36.9 %collective-permute-start.3 = (bf16[256,1408]{1,0:T(8,128)(2,1)}, bf16[256,1408]{1,0:T(8,128)(2,1)}, u32[]{:S(2)}, u32[]{:S(2)}) collective-permute-start(bf16[256,1408]{1,0:T(8,128)(2,1)} %collective-permute-done), channel_id=1, source_target_pairs={{0,16},{16,0},{1,17},{17,1},{2,18},{18,2},{3,19},{19,3},{4,20},{20... | collective-permute-start | bytes 2162696 | tf_op jit(solution)/shard_map/ppermute | solution.py:12
  88.9 22.5 %collective-permute-start.8 = (bf16[176,2048]{1,0:T(8,128)(2,1)}, bf16[176,2048]{1,0:T(8,128)(2,1)}, u32[]{:S(2)}, u32[]{:S(2)}) collective-permute-start(bf16[176,2048]{1,0:T(8,128)(2,1)} %get-tuple-element.27), channel_id=1, source_target_pairs={{0,2},{2,0},{1,3},{3,1},{4,6},{6,4},{5,7},{7,5},{8,10},{10,8},{9,1... | collective-permute-start | bytes 2162696 | tf_op jit(solution)/shard_map/ppermute | solution.py:12
  90.5 33.3 %collective-permute-start.10 = (bf16[176,2048]{1,0:T(8,128)(2,1)}, bf16[176,2048]{1,0:T(8,128)(2,1)}, u32[]{:S(2)}, u32[]{:S(2)}) collective-permute-start(bf16[176,2048]{1,0:T(8,128)(2,1)} %get-tuple-element.28), channel_id=1, source_target_pairs={{0,2},{2,0},{1,3},{3,1},{4,6},{6,4},{5,7},{7,5},{8,10},{10,8},{9,1... | collective-permute-start | bytes 2162696 | tf_op jit(solution)/shard_map/ppermute | solution.py:12
  101.9 44.3 %all-to-all-start.2 = ((bf16[8,36,2048]{2,1,0:T(8,128)(2,1)}), bf16[8,36,2048]{2,1,0:T(8,128)(2,1)S(1)}, u32[]{:S(2)}, u32[]{:S(2)}) async-start(bf16[8,36,2048]{2,1,0:T(8,128)(2,1)} %reshape.53), calls=%async_computation.2 | async-start | bytes 2621440 | tf_op jit(solution)/shard_map/all_to_all | solution.py:91
  107.8 54.2 %collective-permute-start.13 = (bf16[288,1024]{1,0:T(8,128)(2,1)}, bf16[288,1024]{1,0:T(8,128)(2,1)}, u32[]{:S(2)}, u32[]{:S(2)}) collective-permute-start(bf16[288,1024]{1,0:T(8,128)(2,1)} %get-tuple-element.49), channel_id=1, source_target_pairs={{0,2},{2,0},{1,3},{3,1},{4,6},{6,4},{5,7},{7,5},{8,10},{10,8},{9,1... | collective-permute-start | bytes 1769480 | tf_op jit(solution)/shard_map/ppermute | solution.py:12
  111.4 29.3 %collective-permute-start.9 = (bf16[176,2048]{1,0:T(8,128)(2,1)}, bf16[176,2048]{1,0:T(8,128)(2,1)S(1)}, u32[]{:S(2)}, u32[]{:S(2)}) collective-permute-start(bf16[176,2048]{1,0:T(8,128)(2,1)} %collective-permute-done.8), channel_id=1, source_target_pairs={{0,16},{16,0},{1,17},{17,1},{2,18},{18,2},{3,19},{19,3},{4,20},{20... | collective-permute-start | bytes 2162696 | tf_op jit(solution)/shard_map/ppermute | solution.py:12
  123.7 21.6 %collective-permute-start.11 = (bf16[176,2048]{1,0:T(8,128)(2,1)}, bf16[176,2048]{1,0:T(8,128)(2,1)S(1)}, u32[]{:S(2)}, u32[]{:S(2)}) collective-permute-start(bf16[176,2048]{1,0:T(8,128)(2,1)} %collective-permute-done.10), channel_id=1, source_target_pairs={{0,16},{16,0},{1,17},{17,1},{2,18},{18,2},{3,19},{19,3},{4,20},{20... | collective-permute-start | bytes 2162696 | tf_op jit(solution)/shard_map/ppermute | solution.py:12
  131.9 6.7 %copy-start.14 = (f32[288,1408]{1,0:T(8,128)}, f32[288,1408]{1,0:T(8,128)S(1)}, u32[]{:S(2)}) copy-start(f32[288,1408]{1,0:T(8,128)S(1)} %fusion.46) | copy-start | bytes 4866052
  146.5 15.4 %copy-start.10 = (bf16[288,2048]{1,0:T(8,128)(2,1)}, bf16[288,2048]{1,0:T(8,128)(2,1)S(1)}, u32[]{:S(2)}) copy-start(bf16[288,2048]{1,0:T(8,128)(2,1)S(1)} %reshape.54) | copy-start | bytes 3538948
  146.5 29.1 %collective-permute-start.12 = (bf16[288,2048]{1,0:T(8,128)(2,1)S(1)}, bf16[288,2048]{1,0:T(8,128)(2,1)}, u32[]{:S(2)}, u32[]{:S(2)}) collective-permute-start(bf16[288,2048]{1,0:T(8,128)(2,1)S(1)} %reshape.54), channel_id=1, source_target_pairs={{0,2},{2,0},{1,3},{3,1},{4,6},{6,4},{5,7},{7,5},{8,10},{10,8},{9,1... | collective-permute-start | bytes 3538952 | tf_op jit(solution)/shard_map/ppermute | solution.py:12
  153.1 37.0 %all-to-all-start.1 = ((bf16[8,36,2048]{2,1,0:T(8,128)(2,1)}), bf16[8,36,2048]{2,1,0:T(8,128)(2,1)S(1)}, u32[]{:S(2)}, u32[]{:S(2)}) async-start(bf16[8,36,2048]{2,1,0:T(8,128)(2,1)} %reshape.51), calls=%async_computation.1 | async-start | bytes 2621440 | tf_op jit(solution)/shard_map/all_to_all | solution.py:91
  157.9 17.7 %slice-start = ((s8[5767168]{0:T(1024)(128)(4,1)}), s8[4194304]{0:T(1024)(128)(4,1)S(1)}, s32[]{:S(2)}) async-start(s8[5767168]{0:T(1024)(128)(4,1)} %bitcast.52), calls=%async_computation.4 | async-start | bytes 8388608
  160.4 63.2 %collective-permute-start.16 = (bf16[288,704]{1,0:T(8,128)(2,1)}, bf16[288,704]{1,0:T(8,128)(2,1)}, u32[]{:S(2)}, u32[]{:S(2)}) collective-permute-start(bf16[288,704]{1,0:T(8,128)(2,1)} %get-tuple-element.52), channel_id=1, source_target_pairs={{0,2},{2,0},{1,3},{3,1},{4,6},{6,4},{5,7},{7,5},{8,10},{10,8},{9,1... | collective-permute-start | bytes 1216520 | tf_op jit(solution)/shard_map/ppermute | solution.py:12
  161.9 13.6 %slice-start.1 = ((s8[5767168]{0:T(1024)(128)(4,1)}), s8[1572864]{0:T(1024)(128)(4,1)S(1)}, s32[]{:S(2)}) async-start(s8[5767168]{0:T(1024)(128)(4,1)} %bitcast.52), calls=%async_computation.5 | async-start | bytes 3145728
  169.1 33.3 %collective-permute-start.14 = (bf16[288,1408]{1,0:T(8,128)(2,1)}, bf16[288,1408]{1,0:T(8,128)(2,1)}, u32[]{:S(2)}, u32[]{:S(2)}) collective-permute-start(bf16[288,1408]{1,0:T(8,128)(2,1)} %get-tuple-element.33), channel_id=1, source_target_pairs={{0,2},{2,0},{1,3},{3,1},{4,6},{6,4},{5,7},{7,5},{8,10},{10,8},{9,1... | collective-permute-start | bytes 2433032 | tf_op jit(solution)/shard_map/ppermute | solution.py:12
  169.6 48.6 %collective-permute-start.15 = (bf16[288,1408]{1,0:T(8,128)(2,1)}, bf16[288,1408]{1,0:T(8,128)(2,1)}, u32[]{:S(2)}, u32[]{:S(2)}) collective-permute-start(bf16[288,1408]{1,0:T(8,128)(2,1)} %get-tuple-element.40), channel_id=1, source_target_pairs={{0,2},{2,0},{1,3},{3,1},{4,6},{6,4},{5,7},{7,5},{8,10},{10,8},{9,1... | collective-permute-start | bytes 2433032 | tf_op jit(solution)/shard_map/ppermute | solution.py:12
  184.7 9.9 %copy-start.9 = (bf16[288,1024]{1,0:T(8,128)(2,1)S(1)}, bf16[288,1024]{1,0:T(8,128)(2,1)}, u32[]{:S(2)}) copy-start(bf16[288,1024]{1,0:T(8,128)(2,1)} %get-tuple-element.34) | copy-start | bytes 1769476
  190.1 41.7 %all-to-all-start.3 = ((bf16[8,36,2048]{2,1,0:T(8,128)(2,1)}), bf16[8,36,2048]{2,1,0:T(8,128)(2,1)}, u32[]{:S(2)}, u32[]{:S(2)}) async-start(bf16[8,36,2048]{2,1,0:T(8,128)(2,1)} %reshape.55), calls=%async_computation.3 | async-start | bytes 2621440 | tf_op jit(solution)/shard_map/all_to_all | solution.py:91
  207.8 15.8 %copy-start.11 = (bf16[288,2048]{1,0:T(8,128)(2,1)S(1)}, bf16[288,2048]{1,0:T(8,128)(2,1)}, u32[]{:S(2)}) copy-start(bf16[288,2048]{1,0:T(8,128)(2,1)} %copy-done.10) | copy-start | bytes 3538948
  229.8 4.8 %copy-start.1 = (bf16[128,2048]{1,0:T(8,128)(2,1)S(1)}, bf16[128,2048]{1,0:T(8,128)(2,1)}, u32[]{:S(2)}) copy-start(bf16[128,2048]{1,0:T(8,128)(2,1)} %param.7) | copy-start | bytes 1572868
  (6 other events, 14.5 us)

commit v3 on v2

--- a/solution.py
+++ b/solution.py
@@ -101,18 +101,19 @@
         return sent[:1] + [shift(sent[step], "dp", step) for step in range(1, n_replica)]
 
     rows = exchange(send_rows)
-    rows, send_grads, down_mine, gate_fetched[0][-1] = lax.optimization_barrier(
-        (rows, send_grads, down_mine, gate_fetched[0][-1])
+    rows, send_grads, down_mine, gate_fetched = lax.optimization_barrier(
+        (rows, send_grads, down_mine, gate_fetched)
     )
-    grads = exchange(send_grads)
+    up_fetched, _ = lax.optimization_barrier((up_fetched, rows))
+    held_rows, grads = lax.optimization_barrier((rows, exchange(send_grads)))
     down_fetched = fetch(down_mine)
     full_gate = gather_weight(w_gate[0], gate_fetched)
     full_up = gather_weight(w_up[0], up_fetched)
     full_down = gather_weight(w_down[0], down_fetched)
     all_rows = to_replicas(rows, split=True)
     all_grads = to_replicas(grads)
-    gate_pre = dot(rows, full_gate)
-    up_pre = dot(rows, full_up)
+    gate_pre = dot(held_rows, full_gate)
+    up_pre = dot(held_rows, full_up)
     squash = jax.nn.sigmoid(gate_pre)
     active = gate_pre * squash
     hidden, full_down = lax.optimization_barrier(((active * up_pre).astype(BF16), full_down))

time: 236 us -> 251 us (1.064)
  waiting for transfers between devices: 83 us -> 103 us
    all_to_all x4, waiting for transfers between devices: 3.07 us -> 14.8 us  [exchange(): lax.all_to_all(value, ('expert', 'pair'), split_axis=0, concat_axis=0, ti...]
    ppermute x17, waiting for transfers between devices: 79.9 us -> 88 us  [shift(): lax.ppermute(value, axis, [(i, (i + step) % size) for i in range(size)])]
    unnamed x35 -> x49, local copies, waits for them, and re-layouts: 2.73 us -> 5.21 us
  transfers between devices with their start and end apart: 21 -> 21, of which waited for: 10 -> 13; matrix products, arithmetic and copies ran while one was open for 42% -> 37% of each run, Pallas kernels for 0% -> 0%
where the time goes in v3:
time: 251 us; the launch traced here: 250 us
  waiting for transfers between devices  103 us (41%)
  local copies, waits for them, and re-layouts  53.6 us (21%)
  matrix products  53.4 us (21%)
  starting transfers between devices  38.8 us (15%)
    ppermute x17, waiting for transfers between devices, shift(): lax.ppermute(value, axis, [(i, (i + step) % size) for i in range(size)])  88 us
    dot_general x15, matrix products, dot(): lax.dot_general(a, b, (((a_dim,), (b_dim,)), ((), ())), preferred_element...  53.4 us
    all_to_all x4, starting transfers between devices, exchange(): lax.all_to_all(value, ('expert', 'pair'), split_axis=0, concat_axis=0, ti...  21.2 us
    ppermute x17, starting transfers between devices, shift(): lax.ppermute(value, axis, [(i, (i + step) % size) for i in range(size)])  17.7 us
    all_to_all x4, waiting for transfers between devices, exchange(): lax.all_to_all(value, ('expert', 'pair'), split_axis=0, concat_axis=0, ti...  14.8 us
    dynamic_update_slice x6, local copies, waits for them, and re-layouts, gather_weight(): full = lax.dynamic_update_slice_in_dim(full, piece, base + group * share, 0)  10 us
    reshape x4, local copies, waits for them, and re-layouts, exchange(): value = value.reshape(experts, capacity, model_width)  7.05 us
    dynamic_update_slice x6, local copies, waits for them, and re-layouts, gather_weight(): lax.dynamic_update_slice_in_dim(full, other, base + origin * share, 0)  6.66 us
  transfers between devices with their start and end apart: 21, of which 13 were waited for; matrix products, arithmetic and copies ran while one was open for 37% of the time, Pallas kernels for 0%

profile of v3, /device:TPU:0, one launch (start us, length us, event | category | flops | bytes accessed | tf_op | source)
XLA Modules:
  0.0 250.3 jit_solution(1728429737350740874)
XLA Ops:
  0.7 2.6 %dynamic-slice_bitcast_fusion.4 = (bf16[256,1408]{1,0:T(8,128)(2,1)}, bf16[256,1408]{1,0:T(8,128)(2,1)}) fusion(bf16[1,1024,1408]{2,1,0:T(8,128)(2,1)} %param.11, s32[]{:T(128)S(6)} %select_n.62, s32[]{:T(128)S(6)} %select_n.61), kind=kLoop, calls=%fused_computation.46 | loop fusion | bytes 2883592 | tf_op jit(solution)/shard_map/dynamic_slice | solution.py:25
  5.4 2.4 reshape.49
  7.8 6.5 %all-to-all-start = ((bf16[8,36,2048]{2,1,0:T(8,128)(2,1)}), bf16[8,36,2048]{2,1,0:T(8,128)(2,1)}, u32[]{:S(2)}, u32[]{:S(2)}) async-start(bf16[8,36,2048]{2,1,0:T(8,128)(2,1)} %reshape.49), calls=%async_computation | async-start | bytes 2621440 | tf_op jit(solution)/shard_map/all_to_all | solution.py:91
  19.6 2.9 %broadcast.11.clone = bf16[2048,1408]{1,0:T(8,128)(2,1)} broadcast(bf16[]{:T(256)} %constant.54.clone.1), dimensions={} | broadcast | bytes 5767170 | tf_op jit(solution)/shard_map/broadcast.3
  25.2 2.5 copy-done.6
  31.8 14.8 %all-to-all-done = bf16[8,36,2048]{2,1,0:T(8,128)(2,1)} async-done(((bf16[8,36,2048]{2,1,0:T(8,128)(2,1)}), bf16[8,36,2048]{2,1,0:T(8,128)(2,1)}, u32[]{:S(2)}, u32[]{:S(2)}) %all-to-all-start) | async-done | bytes 1179680 | tf_op jit(solution)/shard_map/all_to_all | solution.py:91
  46.6 2.2 reshape.50
  50.5 3.2 %broadcast_in_dim.16 = bf16[1408,2048]{1,0:T(8,128)(2,1)} broadcast(bf16[]{:T(256)} %constant.54.clone.1), dimensions={} | broadcast | bytes 5767170 | tf_op jit(solution)/shard_map/broadcast_in_dim | solution.py:41
  56.7 5.3 %all-to-all-start.1 = ((bf16[8,36,2048]{2,1,0:T(8,128)(2,1)}), bf16[8,36,2048]{2,1,0:T(8,128)(2,1)S(1)}, u32[]{:S(2)}, u32[]{:S(2)}) async-start(bf16[8,36,2048]{2,1,0:T(8,128)(2,1)} %reshape.51), calls=%async_computation.1 | async-start | bytes 2621440 | tf_op jit(solution)/shard_map/all_to_all | solution.py:91
  64.4 15.1 %collective-permute-done.5 = bf16[256,1408]{1,0:T(8,128)(2,1)} collective-permute-done((bf16[256,1408]{1,0:T(8,128)(2,1)}, bf16[256,1408]{1,0:T(8,128)(2,1)}, u32[]{:S(2)}, u32[]{:S(2)}) %collective-permute-start.5) | collective-permute-done | bytes 720928 | tf_op jit(solution)/shard_map/ppermute | solution.py:12
  90.9 2.0 constant_dynamic-update-slice_fusion.9
  92.9 5.8 %collective-permute-done.6 = bf16[256,1408]{1,0:T(8,128)(2,1)S(1)} collective-permute-done((bf16[256,1408]{1,0:T(8,128)(2,1)}, bf16[256,1408]{1,0:T(8,128)(2,1)S(1)}, u32[]{:S(2)}, u32[]{:S(2)}) %collective-permute-start.6) | collective-permute-done | bytes 720928 | tf_op jit(solution)/shard_map/ppermute | solution.py:12
  101.8 14.0 %collective-permute-done.10 = bf16[176,2048]{1,0:T(8,128)(2,1)S(1)} collective-permute-done((bf16[176,2048]{1,0:T(8,128)(2,1)}, bf16[176,2048]{1,0:T(8,128)(2,1)S(1)}, u32[]{:S(2)}, u32[]{:S(2)}) %collective-permute-start.10) | collective-permute-done | bytes 720928 | tf_op jit(solution)/shard_map/ppermute | solution.py:12
  117.2 2.0 constant_dynamic-update-slice_fusion.5
  122.0 7.6 %collective-permute-done.9 = bf16[176,2048]{1,0:T(8,128)(2,1)S(1)} collective-permute-done((bf16[176,2048]{1,0:T(8,128)(2,1)S(1)}, bf16[176,2048]{1,0:T(8,128)(2,1)S(1)}, u32[]{:S(2)}, u32[]{:S(2)}) %collective-permute-start.9) | collective-permute-done | bytes 720928 | tf_op jit(solution)/shard_map/ppermute | solution.py:12
  131.5 12.5 %collective-permute-done.11 = bf16[176,2048]{1,0:T(8,128)(2,1)S(1)} collective-permute-done((bf16[176,2048]{1,0:T(8,128)(2,1)S(1)}, bf16[176,2048]{1,0:T(8,128)(2,1)S(1)}, u32[]{:S(2)}, u32[]{:S(2)}) %collective-permute-start.11) | collective-permute-done | bytes 720928 | tf_op jit(solution)/shard_map/ppermute | solution.py:12
  146.1 5.1 %fusion.46 = f32[288,1408]{1,0:T(8,128)S(1)} fusion(bf16[288,2048]{1,0:T(8,128)(2,1)} %reshape.50, bf16[2048,1408]{1,0:T(8,128)(2,1)} %constant_dynamic-update-slice_fusion.8), kind=kOutput, calls=%fused_computation.96 | convolution fusion | flops 1660944384 | bytes 8568832 | tf_op jit(solution)/shard_map/dot_general | solution.py:56
  151.3 3.3 %multiply_convert_fusion.2 = (bf16[288,1408]{1,0:T(8,128)(2,1)S(1)}, f32[288,1408]{1,0:T(8,128)}) fusion(f32[288,1408]{1,0:T(8,128)S(1)} %fusion.46, bf16[288,2048]{1,0:T(8,128)(2,1)S(1)} %copy-done.10, bf16[2048,1408]{1,0:T(8,128)(2,1)S(1)} %bitcast.53), kind=kOutput, calls=%fused_computation.31 | convolution fusion | flops 1663377408 | bytes 11001856 | tf_op jit(solution)/shard_map/dot_general | solution.py:56
  155.5 4.7 %convolution_convert_fusion.4 = bf16[288,2048]{1,0:T(8,128)(2,1)S(1)} fusion(bf16[288,1408]{1,0:T(8,128)(2,1)S(1)} %get-tuple-element.39, bf16[1408,2048]{1,0:T(8,128)(2,1)} %constant_dynamic-update-slice_fusion), kind=kOutput, calls=%fused_computation.13 | convolution fusion | flops 1661534208 | bytes 7757824 | tf_op jit(solution)/shard_map/dot_general | solution.py:56
  161.4 4.3 %all-to-all-start.2 = ((bf16[8,36,2048]{2,1,0:T(8,128)(2,1)}), bf16[8,36,2048]{2,1,0:T(8,128)(2,1)S(1)}, u32[]{:S(2)}, u32[]{:S(2)}) async-start(bf16[8,36,2048]{2,1,0:T(8,128)(2,1)} %reshape.53), calls=%async_computation.2 | async-start | bytes 2621440 | tf_op jit(solution)/shard_map/all_to_all | solution.py:91
  167.2 7.5 %multiply_convert_fusion.1 = (bf16[288,1408]{1,0:T(8,128)(2,1)}, bf16[288,1408]{1,0:T(8,128)(2,1)}) fusion(f32[288,1408]{1,0:T(8,128)} %get-tuple-element.68, f32[288,1408]{1,0:T(8,128)} %copy-done.19, bf16[288,2048]{1,0:T(8,128)(2,1)} %reshape.52, bf16[1408,2048]{1,0:T(8,128)(2,1)} %constant_dynamic-update-slice_fusion), kind=kOutput, calls=%fused_computation.30 | convolution fusion | flops 1665810432 | bytes 11812864 | tf_op jit(solution)/shard_map/dot_general | solution.py:56
  178.4 3.2 %fusion.47 = f32[288,2048]{1,0:T(8,128)S(1)} fusion(bf16[288,1408]{1,0:T(8,128)(2,1)} %get-tuple-element.51, bf16[2048,1408]{1,0:T(8,128)(2,1)S(1)} %bitcast.55), kind=kOutput, calls=%fused_computation.97 | convolution fusion | flops 1660944384 | bytes 8937472 | tf_op jit(solution)/shard_map/dot_general | solution.py:56
  181.6 13.0 %collective-permute-done.12 = bf16[288,2048]{1,0:T(8,128)(2,1)S(1)} collective-permute-done((bf16[288,2048]{1,0:T(8,128)(2,1)}, bf16[288,2048]{1,0:T(8,128)(2,1)S(1)}, u32[]{:S(2)}, u32[]{:S(2)}) %collective-permute-start.12) | collective-permute-done | bytes 1179680 | tf_op jit(solution)/shard_map/ppermute | solution.py:12
  195.7 5.9 %fusion.4 = bf16[288,2048]{1,0:T(8,128)(2,1)} fusion(f32[288,2048]{1,0:T(8,128)S(1)} %fusion.47, bf16[288,1408]{1,0:T(8,128)(2,1)} %get-tuple-element.43, bf16[2048,1408]{1,0:T(8,128)(2,1)} %constant_dynamic-update-slice_fusion.8), kind=kOutput, calls=%fused_computation.14 | convolution fusion | flops 1662124032 | bytes 10117120 | tf_op jit(solution)/shard_map/dot_general | solution.py:56
  201.6 2.3 reshape.55
  203.9 5.2 %all-to-all-start.3 = ((bf16[8,36,2048]{2,1,0:T(8,128)(2,1)}), bf16[8,36,2048]{2,1,0:T(8,128)(2,1)}, u32[]{:S(2)}, u32[]{:S(2)}) async-start(bf16[8,36,2048]{2,1,0:T(8,128)(2,1)} %reshape.55), calls=%async_computation.3 | async-start | bytes 2621440 | tf_op jit(solution)/shard_map/all_to_all | solution.py:91
  212.1 5.3 %fusion = bf16[1,1024,1408]{2,1,0:T(8,128)(2,1)} fusion(bf16[576,1024]{1,0:T(8,128)(2,1)S(1)} %constant_dynamic-update-slice_fusion.12, bf16[288,1408]{1,0:T(8,128)(2,1)} %collective-permute-done.14, bf16[288,1408]{1,0:T(8,128)(2,1)} %get-tuple-element.43), kind=kOutput, calls=%fused_computation.3 | convolution fusion | flops 1665630208 | bytes 5685248 | tf_op jit(solution)/shard_map/dot_general | solution.py:56
  217.5 12.0 %collective-permute-done.15 = bf16[288,1408]{1,0:T(8,128)(2,1)} collective-permute-done((bf16[288,1408]{1,0:T(8,128)(2,1)}, bf16[288,1408]{1,0:T(8,128)(2,1)}, u32[]{:S(2)}, u32[]{:S(2)}) %collective-permute-start.15) | collective-permute-done | bytes 811040 | tf_op jit(solution)/shard_map/ppermute | solution.py:12
  229.5 5.3 %fusion.1 = bf16[1,1024,1408]{2,1,0:T(8,128)(2,1)} fusion(bf16[576,1024]{1,0:T(8,128)(2,1)S(1)} %constant_dynamic-update-slice_fusion.12, bf16[288,1408]{1,0:T(8,128)(2,1)} %collective-permute-done.15, bf16[288,1408]{1,0:T(8,128)(2,1)} %get-tuple-element.51), kind=kOutput, calls=%fused_computation.4 | convolution fusion | flops 1665630208 | bytes 5685248 | tf_op jit(solution)/shard_map/dot_general | solution.py:56
  234.8 3.8 %collective-permute-done.16 = bf16[288,704]{1,0:T(8,128)(2,1)} collective-permute-done((bf16[288,704]{1,0:T(8,128)(2,1)}, bf16[288,704]{1,0:T(8,128)(2,1)}, u32[]{:S(2)}, u32[]{:S(2)}) %collective-permute-start.16) | collective-permute-done | bytes 405536 | tf_op jit(solution)/shard_map/ppermute | solution.py:12
  238.6 5.0 %fusion.2 = bf16[1,704,2048]{2,1,0:T(8,128)(2,1)} fusion(bf16[288,2048]{1,0:T(8,128)(2,1)S(1)} %copy-done.18, bf16[288,2048]{1,0:T(8,128)(2,1)S(1)} %copy-done.12, bf16[288,704]{1,0:T(8,128)(2,1)} %collective-permute-done.16, bf16[288,704]{1,0:T(8,128)(2,1)S(1)} %get-tuple-element.61), kind=kOutput, calls=%fused_computation.5 | convolution fusion | flops 1668726784 | bytes 6053888 | tf_op jit(solution)/shard_map/dot_general | solution.py:56
  244.4 2.6 %fusion.17 = (f32[128]{0:T(128)S(1)}, f32[128]{0:T(128)S(1)}, bf16[128,2048]{1,0:T(8,128)(2,1)}) fusion(bf16[128,2048]{1,0:T(8,128)(2,1)} %param.10, f32[128,2048]{1,0:T(8,128)S(1)} %fusion.28, f32[128]{0:T(128)S(1)} %get-tuple-element.63, f32[128]{0:T(128)S(1)} %get-tuple-element.64, bf16[288,2048]{1,0:T(8,128)(2,1)S(1)} %reshape.54, ...), kind=kOutput, calls=%fused_computation.36 | convolution fusion | flops 153390848 | bytes 3279360 | tf_op jit(solution)/shard_map/dot_general | solution.py:56
  (117 shorter events, 59.3 us)
Async XLA Ops:
  5.4 10.9 %copy-start.3 = (bf16[1,1024,1408]{2,1,0:T(8,128)(2,1)S(1)}, bf16[1,1024,1408]{2,1,0:T(8,128)(2,1)}, u32[]{:S(2)}) copy-start(bf16[1,1024,1408]{2,1,0:T(8,128)(2,1)} %param.12) | copy-start | bytes 8650756
  7.8 11.8 %copy-start.16 = (f32[128,2]{0,1:T(2,128)S(1)}, f32[128,2]{0,1:T(2,128)}, u32[]{:S(2)}) copy-start(f32[128,2]{0,1:T(2,128)} %param.9) | copy-start | bytes 3076
  7.8 38.8 %all-to-all-start = ((bf16[8,36,2048]{2,1,0:T(8,128)(2,1)}), bf16[8,36,2048]{2,1,0:T(8,128)(2,1)}, u32[]{:S(2)}, u32[]{:S(2)}) async-start(bf16[8,36,2048]{2,1,0:T(8,128)(2,1)} %reshape.49), calls=%async_computation | async-start | bytes 2621440 | tf_op jit(solution)/shard_map/all_to_all | solution.py:91
  14.3 34.5 %collective-permute-start = (bf16[256,1408]{1,0:T(8,128)(2,1)}, bf16[256,1408]{1,0:T(8,128)(2,1)}, u32[]{:S(2)}, u32[]{:S(2)}) collective-permute-start(bf16[256,1408]{1,0:T(8,128)(2,1)} %get-tuple-element.28), channel_id=1, source_target_pairs={{0,2},{2,0},{1,3},{3,1},{4,6},{6,4},{5,7},{7,5},{8,10},{10,8},{9,1... | collective-permute-start | bytes 2162696 | tf_op jit(solution)/shard_map/ppermute | solution.py:12
  15.8 33.2 %collective-permute-start.1 = (bf16[256,1408]{1,0:T(8,128)(2,1)}, bf16[256,1408]{1,0:T(8,128)(2,1)}, u32[]{:S(2)}, u32[]{:S(2)}) collective-permute-start(bf16[256,1408]{1,0:T(8,128)(2,1)} %get-tuple-element.29), channel_id=1, source_target_pairs={{0,2},{2,0},{1,3},{3,1},{4,6},{6,4},{5,7},{7,5},{8,10},{10,8},{9,1... | collective-permute-start | bytes 2162696 | tf_op jit(solution)/shard_map/ppermute | solution.py:12
  17.6 46.9 %collective-permute-start.4 = (bf16[256,1408]{1,0:T(8,128)(2,1)}, bf16[256,1408]{1,0:T(8,128)(2,1)}, u32[]{:S(2)}, u32[]{:S(2)}) collective-permute-start(bf16[256,1408]{1,0:T(8,128)(2,1)} %get-tuple-element.53), channel_id=1, source_target_pairs={{0,2},{2,0},{1,3},{3,1},{4,6},{6,4},{5,7},{7,5},{8,10},{10,8},{9,1... | collective-permute-start | bytes 2162696 | tf_op jit(solution)/shard_map/ppermute | solution.py:12
  19.0 60.5 %collective-permute-start.5 = (bf16[256,1408]{1,0:T(8,128)(2,1)}, bf16[256,1408]{1,0:T(8,128)(2,1)}, u32[]{:S(2)}, u32[]{:S(2)}) collective-permute-start(bf16[256,1408]{1,0:T(8,128)(2,1)} %get-tuple-element.52), channel_id=1, source_target_pairs={{0,2},{2,0},{1,3},{3,1},{4,6},{6,4},{5,7},{7,5},{8,10},{10,8},{9,1... | collective-permute-start | bytes 2162696 | tf_op jit(solution)/shard_map/ppermute | solution.py:12
  49.0 39.3 %collective-permute-start.2 = (bf16[256,1408]{1,0:T(8,128)(2,1)}, bf16[256,1408]{1,0:T(8,128)(2,1)}, u32[]{:S(2)}, u32[]{:S(2)}) collective-permute-start(bf16[256,1408]{1,0:T(8,128)(2,1)} %collective-permute-done), channel_id=1, source_target_pairs={{0,16},{16,0},{1,17},{17,1},{2,18},{18,2},{3,19},{19,3},{4,20},{20... | collective-permute-start | bytes 2162696 | tf_op jit(solution)/shard_map/ppermute | solution.py:12
  56.7 26.4 %copy-start.9 = (bf16[288,2048]{1,0:T(8,128)(2,1)S(1)}, bf16[288,2048]{1,0:T(8,128)(2,1)}, u32[]{:S(2)}) copy-start(bf16[288,2048]{1,0:T(8,128)(2,1)} %reshape.50) | copy-start | bytes 3538948
  56.7 88.3 %all-to-all-start.1 = ((bf16[8,36,2048]{2,1,0:T(8,128)(2,1)}), bf16[8,36,2048]{2,1,0:T(8,128)(2,1)S(1)}, u32[]{:S(2)}, u32[]{:S(2)}) async-start(bf16[8,36,2048]{2,1,0:T(8,128)(2,1)} %reshape.51), calls=%async_computation.1 | async-start | bytes 2621440 | tf_op jit(solution)/shard_map/all_to_all | solution.py:91
  61.9 57.3 %collective-permute-start.3 = (bf16[256,1408]{1,0:T(8,128)(2,1)}, bf16[256,1408]{1,0:T(8,128)(2,1)S(1)}, u32[]{:S(2)}, u32[]{:S(2)}) collective-permute-start(bf16[256,1408]{1,0:T(8,128)(2,1)} %collective-permute-done.1), channel_id=1, source_target_pairs={{0,16},{16,0},{1,17},{17,1},{2,18},{18,2},{3,19},{19,3},{4,20},{20... | collective-permute-start | bytes 2162696 | tf_op jit(solution)/shard_map/ppermute | solution.py:12
  79.5 19.3 %collective-permute-start.6 = (bf16[256,1408]{1,0:T(8,128)(2,1)}, bf16[256,1408]{1,0:T(8,128)(2,1)S(1)}, u32[]{:S(2)}, u32[]{:S(2)}) collective-permute-start(bf16[256,1408]{1,0:T(8,128)(2,1)} %collective-permute-done.4), channel_id=1, source_target_pairs={{0,16},{16,0},{1,17},{17,1},{2,18},{18,2},{3,19},{19,3},{4,20},{20... | collective-permute-start | bytes 2162696 | tf_op jit(solution)/shard_map/ppermute | solution.py:12
  81.0 19.3 %collective-permute-start.8 = (bf16[176,2048]{1,0:T(8,128)(2,1)}, bf16[176,2048]{1,0:T(8,128)(2,1)S(1)}, u32[]{:S(2)}, u32[]{:S(2)}) collective-permute-start(bf16[176,2048]{1,0:T(8,128)(2,1)} %get-tuple-element.37), channel_id=1, source_target_pairs={{0,2},{2,0},{1,3},{3,1},{4,6},{6,4},{5,7},{7,5},{8,10},{10,8},{9,1... | collective-permute-start | bytes 2162696 | tf_op jit(solution)/shard_map/ppermute | solution.py:12
  82.5 33.2 %collective-permute-start.10 = (bf16[176,2048]{1,0:T(8,128)(2,1)}, bf16[176,2048]{1,0:T(8,128)(2,1)S(1)}, u32[]{:S(2)}, u32[]{:S(2)}) collective-permute-start(bf16[176,2048]{1,0:T(8,128)(2,1)} %get-tuple-element.38), channel_id=1, source_target_pairs={{0,2},{2,0},{1,3},{3,1},{4,6},{6,4},{5,7},{7,5},{8,10},{10,8},{9,1... | collective-permute-start | bytes 2162696 | tf_op jit(solution)/shard_map/ppermute | solution.py:12
  88.3 31.9 %collective-permute-start.7 = (bf16[256,1408]{1,0:T(8,128)(2,1)}, bf16[256,1408]{1,0:T(8,128)(2,1)S(1)}, u32[]{:S(2)}, u32[]{:S(2)}) collective-permute-start(bf16[256,1408]{1,0:T(8,128)(2,1)} %collective-permute-done.5), channel_id=1, source_target_pairs={{0,16},{16,0},{1,17},{17,1},{2,18},{18,2},{3,19},{19,3},{4,20},{20... | collective-permute-start | bytes 2162696 | tf_op jit(solution)/shard_map/ppermute | solution.py:12
  98.8 68.4 %collective-permute-start.13 = (bf16[288,1024]{1,0:T(8,128)(2,1)}, bf16[288,1024]{1,0:T(8,128)(2,1)}, u32[]{:S(2)}, u32[]{:S(2)}) collective-permute-start(bf16[288,1024]{1,0:T(8,128)(2,1)} %get-tuple-element.59), channel_id=1, source_target_pairs={{0,2},{2,0},{1,3},{3,1},{4,6},{6,4},{5,7},{7,5},{8,10},{10,8},{9,1... | collective-permute-start | bytes 1769480 | tf_op jit(solution)/shard_map/ppermute | solution.py:12
  100.3 29.3 %collective-permute-start.9 = (bf16[176,2048]{1,0:T(8,128)(2,1)S(1)}, bf16[176,2048]{1,0:T(8,128)(2,1)S(1)}, u32[]{:S(2)}, u32[]{:S(2)}) collective-permute-start(bf16[176,2048]{1,0:T(8,128)(2,1)S(1)} %collective-permute-done.8), channel_id=1, source_target_pairs={{0,16},{16,0},{1,17},{17,1},{2,18},{18,2},{3,19},{19,3},{4,20},{20... | collective-permute-start | bytes 2162696 | tf_op jit(solution)/shard_map/ppermute | solution.py:12
  115.8 28.3 %collective-permute-start.11 = (bf16[176,2048]{1,0:T(8,128)(2,1)S(1)}, bf16[176,2048]{1,0:T(8,128)(2,1)S(1)}, u32[]{:S(2)}, u32[]{:S(2)}) collective-permute-start(bf16[176,2048]{1,0:T(8,128)(2,1)S(1)} %collective-permute-done.10), channel_id=1, source_target_pairs={{0,16},{16,0},{1,17},{17,1},{2,18},{18,2},{3,19},{19,3},{4,20},{20... | collective-permute-start | bytes 2162696 | tf_op jit(solution)/shard_map/ppermute | solution.py:12
  145.0 6.3 %slice-start = ((s8[5767168]{0:T(1024)(128)(4,1)}), s8[1572864]{0:T(1024)(128)(4,1)S(1)}, s32[]{:S(2)}) async-start(s8[5767168]{0:T(1024)(128)(4,1)} %bitcast.52), calls=%async_computation.4 | async-start | bytes 3145728
  161.4 17.0 %slice-start.2 = ((s8[5767168]{0:T(1024)(128)(4,1)}), s8[1572864]{0:T(1024)(128)(4,1)S(1)}, s32[]{:S(2)}) async-start(s8[5767168]{0:T(1024)(128)(4,1)} %bitcast.54), calls=%async_computation.6 | async-start | bytes 3145728
  161.4 42.5 %all-to-all-start.2 = ((bf16[8,36,2048]{2,1,0:T(8,128)(2,1)}), bf16[8,36,2048]{2,1,0:T(8,128)(2,1)S(1)}, u32[]{:S(2)}, u32[]{:S(2)}) async-start(bf16[8,36,2048]{2,1,0:T(8,128)(2,1)} %reshape.53), calls=%async_computation.2 | async-start | bytes 2621440 | tf_op jit(solution)/shard_map/all_to_all | solution.py:91
  165.7 29.0 %collective-permute-start.12 = (bf16[288,2048]{1,0:T(8,128)(2,1)}, bf16[288,2048]{1,0:T(8,128)(2,1)S(1)}, u32[]{:S(2)}, u32[]{:S(2)}) collective-permute-start(bf16[288,2048]{1,0:T(8,128)(2,1)} %reshape.52), channel_id=1, source_target_pairs={{0,2},{2,0},{1,3},{3,1},{4,6},{6,4},{5,7},{7,5},{8,10},{10,8},{9,1... | collective-permute-start | bytes 3538952 | tf_op jit(solution)/shard_map/ppermute | solution.py:12
  167.2 9.6 %copy-start.14 = (bf16[288,1408]{1,0:T(8,128)(2,1)S(1)}, bf16[288,1408]{1,0:T(8,128)(2,1)}, u32[]{:S(2)}) copy-start(bf16[288,1408]{1,0:T(8,128)(2,1)} %copy-done.13) | copy-start | bytes 2433028
  167.2 11.3 %slice-start.3 = ((s8[5767168]{0:T(1024)(128)(4,1)}), s8[4194304]{0:T(1024)(128)(4,1)S(1)}, s32[]{:S(2)}) async-start(s8[5767168]{0:T(1024)(128)(4,1)} %bitcast.54), calls=%async_computation.7 | async-start | bytes 8388608
  174.7 37.4 %collective-permute-start.14 = (bf16[288,1408]{1,0:T(8,128)(2,1)}, bf16[288,1408]{1,0:T(8,128)(2,1)}, u32[]{:S(2)}, u32[]{:S(2)}) collective-permute-start(bf16[288,1408]{1,0:T(8,128)(2,1)} %get-tuple-element.43), channel_id=1, source_target_pairs={{0,2},{2,0},{1,3},{3,1},{4,6},{6,4},{5,7},{7,5},{8,10},{10,8},{9,1... | collective-permute-start | bytes 2433032 | tf_op jit(solution)/shard_map/ppermute | solution.py:12
  175.2 54.3 %collective-permute-start.15 = (bf16[288,1408]{1,0:T(8,128)(2,1)}, bf16[288,1408]{1,0:T(8,128)(2,1)}, u32[]{:S(2)}, u32[]{:S(2)}) collective-permute-start(bf16[288,1408]{1,0:T(8,128)(2,1)} %get-tuple-element.51), channel_id=1, source_target_pairs={{0,2},{2,0},{1,3},{3,1},{4,6},{6,4},{5,7},{7,5},{8,10},{10,8},{9,1... | collective-permute-start | bytes 2433032 | tf_op jit(solution)/shard_map/ppermute | solution.py:12
  177.9 60.7 %collective-permute-start.16 = (bf16[288,704]{1,0:T(8,128)(2,1)}, bf16[288,704]{1,0:T(8,128)(2,1)}, u32[]{:S(2)}, u32[]{:S(2)}) collective-permute-start(bf16[288,704]{1,0:T(8,128)(2,1)} %get-tuple-element.62), channel_id=1, source_target_pairs={{0,2},{2,0},{1,3},{3,1},{4,6},{6,4},{5,7},{7,5},{8,10},{10,8},{9,1... | collective-permute-start | bytes 1216520 | tf_op jit(solution)/shard_map/ppermute | solution.py:12
  201.6 7.5 %copy-start.11 = (bf16[288,1024]{1,0:T(8,128)(2,1)S(1)}, bf16[288,1024]{1,0:T(8,128)(2,1)}, u32[]{:S(2)}) copy-start(bf16[288,1024]{1,0:T(8,128)(2,1)} %get-tuple-element.44) | copy-start | bytes 1769476
  203.9 43.7 %all-to-all-start.3 = ((bf16[8,36,2048]{2,1,0:T(8,128)(2,1)}), bf16[8,36,2048]{2,1,0:T(8,128)(2,1)}, u32[]{:S(2)}, u32[]{:S(2)}) async-start(bf16[8,36,2048]{2,1,0:T(8,128)(2,1)} %reshape.55), calls=%async_computation.3 | async-start | bytes 2621440 | tf_op jit(solution)/shard_map/all_to_all | solution.py:91
  217.5 21.1 %copy-start.12 = (bf16[288,2048]{1,0:T(8,128)(2,1)S(1)}, bf16[288,2048]{1,0:T(8,128)(2,1)}, u32[]{:S(2)}) copy-start(bf16[288,2048]{1,0:T(8,128)(2,1)} %reshape.52) | copy-start | bytes 3538948
  217.5 21.1 %copy-start.18 = (bf16[288,2048]{1,0:T(8,128)(2,1)S(1)}, bf16[288,2048]{1,0:T(8,128)(2,1)}, u32[]{:S(2)}) copy-start(bf16[288,2048]{1,0:T(8,128)(2,1)} %copy-done.17) | copy-start | bytes 3538948
  244.4 5.9 %copy-start.1 = (bf16[128,2048]{1,0:T(8,128)(2,1)S(1)}, bf16[128,2048]{1,0:T(8,128)(2,1)}, u32[]{:S(2)}) copy-start(bf16[128,2048]{1,0:T(8,128)(2,1)} %param.7) | copy-start | bytes 1572868
  (13 other events, 38.5 us)

commit v4 on v2

--- a/solution.py
+++ b/solution.py
@@ -101,9 +101,10 @@
         return sent[:1] + [shift(sent[step], "dp", step) for step in range(1, n_replica)]
 
     rows = exchange(send_rows)
-    rows, send_grads, down_mine, gate_fetched[0][-1] = lax.optimization_barrier(
-        (rows, send_grads, down_mine, gate_fetched[0][-1])
+    rows, send_grads, down_mine, gate_fetched = lax.optimization_barrier(
+        (rows, send_grads, down_mine, gate_fetched)
     )
+    up_fetched, _ = lax.optimization_barrier((up_fetched, rows))
     grads = exchange(send_grads)
     down_fetched = fetch(down_mine)
     full_gate = gather_weight(w_gate[0], gate_fetched)
@@ -125,8 +126,7 @@
     all_gate = to_replicas(gate_grad)
     all_up = to_replicas(up_grad)
     all_hidden = to_replicas(hidden, split=True)
-    all_grads, held_gate = lax.optimization_barrier((all_grads, gate_grad))
-    input_grad = (dot(held_gate, full_gate, 1, 1) + dot(up_grad, full_up, 1, 1)).astype(BF16)
+    input_grad = (dot(gate_grad, full_gate, 1, 1) + dot(up_grad, full_up, 1, 1)).astype(BF16)
     back_grad = exchange(input_grad)
 
     joined = [jnp.concatenate(v, 0) for v in (all_rows, all_hidden, all_gate, all_up, all_grads)]

time: 236 us -> 247 us (1.047)
  waiting for transfers between devices: 83 us -> 101 us
  matrix products: 55.5 us -> 51.5 us
  starting transfers between devices: 40.1 us -> 37.6 us
    all_to_all x4, waiting for transfers between devices: 3.07 us -> 23.7 us  [exchange(): lax.all_to_all(value, ('expert', 'pair'), split_axis=0, concat_axis=0, ti...]
    dot_general x15, matrix products: 55.5 us -> 51.5 us  [dot(): lax.dot_general(a, b, (((a_dim,), (b_dim,)), ((), ())), preferred_element...]
  transfers between devices with their start and end apart: 21 -> 21, of which waited for: 10 -> 10; matrix products, arithmetic and copies ran while one was open for 42% -> 38% of each run, Pallas kernels for 0% -> 0%
where the time goes in v4:
time: 247 us; the launch traced here: 246 us
  waiting for transfers between devices  101 us (41%)
  local copies, waits for them, and re-layouts  54 us (22%)
  matrix products  51.5 us (21%)
  starting transfers between devices  37.6 us (15%)
    ppermute x17, waiting for transfers between devices, shift(): lax.ppermute(value, axis, [(i, (i + step) % size) for i in range(size)])  77.5 us
    dot_general x15, matrix products, dot(): lax.dot_general(a, b, (((a_dim,), (b_dim,)), ((), ())), preferred_element...  51.5 us
    all_to_all x4, waiting for transfers between devices, exchange(): lax.all_to_all(value, ('expert', 'pair'), split_axis=0, concat_axis=0, ti...  23.7 us
    all_to_all x4, starting transfers between devices, exchange(): lax.all_to_all(value, ('expert', 'pair'), split_axis=0, concat_axis=0, ti...  19.9 us
    ppermute x17, starting transfers between devices, shift(): lax.ppermute(value, axis, [(i, (i + step) % size) for i in range(size)])  17.7 us
    dynamic_update_slice x6, local copies, waits for them, and re-layouts, gather_weight(): full = lax.dynamic_update_slice_in_dim(full, piece, base + group * share, 0)  12.6 us
    dynamic_update_slice x6, local copies, waits for them, and re-layouts, gather_weight(): lax.dynamic_update_slice_in_dim(full, other, base + origin * share, 0)  8.2 us
    reshape x4, local copies, waits for them, and re-layouts, exchange(): value = value.reshape(experts, capacity, model_width)  5.98 us
  transfers between devices with their start and end apart: 21, of which 10 were waited for; matrix products, arithmetic and copies ran while one was open for 38% of the time, Pallas kernels for 0%

profile of v4, /device:TPU:0, one launch (start us, length us, event | category | flops | bytes accessed | tf_op | source)
XLA Modules:
  0.0 246.1 jit_solution(1194950865601943803)
XLA Ops:
  0.7 2.6 %dynamic-slice_bitcast_fusion.4 = (bf16[256,1408]{1,0:T(8,128)(2,1)}, bf16[256,1408]{1,0:T(8,128)(2,1)}) fusion(bf16[1,1024,1408]{2,1,0:T(8,128)(2,1)} %param.11, s32[]{:T(128)S(6)} %select_n.62, s32[]{:T(128)S(6)} %select_n.61), kind=kLoop, calls=%fused_computation.46 | loop fusion | bytes 2883592 | tf_op jit(solution)/shard_map/dynamic_slice | solution.py:25
  5.4 2.4 reshape.49
  7.8 6.5 %all-to-all-start = ((bf16[8,36,2048]{2,1,0:T(8,128)(2,1)}), bf16[8,36,2048]{2,1,0:T(8,128)(2,1)}, u32[]{:S(2)}, u32[]{:S(2)}) async-start(bf16[8,36,2048]{2,1,0:T(8,128)(2,1)} %reshape.49), calls=%async_computation | async-start | bytes 2621440 | tf_op jit(solution)/shard_map/all_to_all | solution.py:91
  19.6 2.9 %broadcast.11.clone = bf16[2048,1408]{1,0:T(8,128)(2,1)} broadcast(bf16[]{:T(256)} %constant.54.clone.1), dimensions={} | broadcast | bytes 5767170 | tf_op jit(solution)/shard_map/broadcast.3
  25.2 2.5 %copy-done.6 = bf16[2048,1408]{1,0:T(8,128)(2,1)} copy-done((bf16[2048,1408]{1,0:T(8,128)(2,1)}, bf16[2048,1408]{1,0:T(8,128)(2,1)S(1)}, u32[]{:S(2)}) %copy-start.6) | copy-done | bytes 5767192
  31.9 14.7 %all-to-all-done = bf16[8,36,2048]{2,1,0:T(8,128)(2,1)} async-done(((bf16[8,36,2048]{2,1,0:T(8,128)(2,1)}), bf16[8,36,2048]{2,1,0:T(8,128)(2,1)}, u32[]{:S(2)}, u32[]{:S(2)}) %all-to-all-start) | async-done | bytes 1179680 | tf_op jit(solution)/shard_map/all_to_all | solution.py:91
  50.5 3.2 %broadcast_in_dim.16 = bf16[1408,2048]{1,0:T(8,128)(2,1)} broadcast(bf16[]{:T(256)} %constant.54.clone.1), dimensions={} | broadcast | bytes 5767170 | tf_op jit(solution)/shard_map/broadcast_in_dim | solution.py:41
  56.0 8.5 %collective-permute-done.4 = bf16[256,1408]{1,0:T(8,128)(2,1)} collective-permute-done((bf16[256,1408]{1,0:T(8,128)(2,1)}, bf16[256,1408]{1,0:T(8,128)(2,1)}, u32[]{:S(2)}, u32[]{:S(2)}) %collective-permute-start.4) | collective-permute-done | bytes 720928 | tf_op jit(solution)/shard_map/ppermute | solution.py:12
  64.4 15.1 %collective-permute-done.5 = bf16[256,1408]{1,0:T(8,128)(2,1)} collective-permute-done((bf16[256,1408]{1,0:T(8,128)(2,1)}, bf16[256,1408]{1,0:T(8,128)(2,1)}, u32[]{:S(2)}, u32[]{:S(2)}) %collective-permute-start.5) | collective-permute-done | bytes 720928 | tf_op jit(solution)/shard_map/ppermute | solution.py:12
  84.2 4.7 %all-to-all-start.2 = ((bf16[8,36,2048]{2,1,0:T(8,128)(2,1)}), bf16[8,36,2048]{2,1,0:T(8,128)(2,1)S(1)}, u32[]{:S(2)}, u32[]{:S(2)}) async-start(bf16[8,36,2048]{2,1,0:T(8,128)(2,1)} %reshape.53), calls=%async_computation.2 | async-start | bytes 2621440 | tf_op jit(solution)/shard_map/all_to_all | solution.py:91
  94.7 2.0 constant_dynamic-update-slice_fusion.10
  96.7 2.0 constant_dynamic-update-slice_fusion.9
  101.9 14.0 %collective-permute-done.10 = bf16[176,2048]{1,0:T(8,128)(2,1)} collective-permute-done((bf16[176,2048]{1,0:T(8,128)(2,1)}, bf16[176,2048]{1,0:T(8,128)(2,1)}, u32[]{:S(2)}, u32[]{:S(2)}) %collective-permute-start.10) | collective-permute-done | bytes 720928 | tf_op jit(solution)/shard_map/ppermute | solution.py:12
  116.3 2.1 constant_dynamic-update-slice_fusion.6
  120.4 2.2 constant_dynamic-update-slice_fusion.8
  122.6 4.7 %fusion.46 = f32[288,1408]{1,0:T(8,128)S(1)} fusion(bf16[288,2048]{1,0:T(8,128)(2,1)S(1)} %reshape.50, bf16[2048,1408]{1,0:T(8,128)(2,1)} %constant_dynamic-update-slice_fusion.8), kind=kOutput, calls=%fused_computation.96 | convolution fusion | flops 1660944384 | bytes 8568832 | tf_op jit(solution)/shard_map/dot_general | solution.py:56
  127.5 3.4 %multiply_convert_fusion.2 = (bf16[288,1408]{1,0:T(8,128)(2,1)S(1)}, f32[288,1408]{1,0:T(8,128)}) fusion(f32[288,1408]{1,0:T(8,128)S(1)} %fusion.46, bf16[288,2048]{1,0:T(8,128)(2,1)S(1)} %reshape.50, bf16[2048,1408]{1,0:T(8,128)(2,1)S(1)} %constant_dynamic-update-slice_fusion.4), kind=kOutput, calls=%fused_computation.31 | convolution fusion | flops 1663377408 | bytes 11001856 | tf_op jit(solution)/shard_map/dot_general | solution.py:56
  131.0 2.4 constant_dynamic-update-slice_fusion.3
  134.2 2.1 constant_dynamic-update-slice_fusion.1
  136.3 7.5 %collective-permute-done.11 = bf16[176,2048]{1,0:T(8,128)(2,1)S(1)} collective-permute-done((bf16[176,2048]{1,0:T(8,128)(2,1)}, bf16[176,2048]{1,0:T(8,128)(2,1)S(1)}, u32[]{:S(2)}, u32[]{:S(2)}) %collective-permute-start.11) | collective-permute-done | bytes 720928 | tf_op jit(solution)/shard_map/ppermute | solution.py:12
  144.7 4.7 %convolution_convert_fusion.4 = bf16[288,2048]{1,0:T(8,128)(2,1)S(1)} fusion(bf16[288,1408]{1,0:T(8,128)(2,1)S(1)} %get-tuple-element.32, bf16[1408,2048]{1,0:T(8,128)(2,1)} %constant_dynamic-update-slice_fusion), kind=kOutput, calls=%fused_computation.13 | convolution fusion | flops 1661534208 | bytes 7757824 | tf_op jit(solution)/shard_map/dot_general | solution.py:56
  150.7 4.9 %all-to-all-start.1 = ((bf16[8,36,2048]{2,1,0:T(8,128)(2,1)}), bf16[8,36,2048]{2,1,0:T(8,128)(2,1)}, u32[]{:S(2)}, u32[]{:S(2)}) async-start(bf16[8,36,2048]{2,1,0:T(8,128)(2,1)} %reshape.51), calls=%async_computation.1 | async-start | bytes 2621440 | tf_op jit(solution)/shard_map/all_to_all | solution.py:91
  159.9 7.6 %multiply_convert_fusion.1 = (bf16[288,1408]{1,0:T(8,128)(2,1)}, bf16[288,1408]{1,0:T(8,128)(2,1)}) fusion(f32[288,1408]{1,0:T(8,128)} %get-tuple-element.58, f32[288,1408]{1,0:T(8,128)} %copy-done.17, bf16[288,2048]{1,0:T(8,128)(2,1)} %reshape.54, bf16[1408,2048]{1,0:T(8,128)(2,1)} %constant_dynamic-update-slice_fusion), kind=kOutput, calls=%fused_computation.30 | convolution fusion | flops 1665810432 | bytes 11812864 | tf_op jit(solution)/shard_map/dot_general | solution.py:56
  169.5 3.2 %fusion.47 = f32[288,2048]{1,0:T(8,128)S(1)} fusion(bf16[288,1408]{1,0:T(8,128)(2,1)} %get-tuple-element.41, bf16[2048,1408]{1,0:T(8,128)(2,1)S(1)} %bitcast.55), kind=kOutput, calls=%fused_computation.97 | convolution fusion | flops 1660944384 | bytes 8937472 | tf_op jit(solution)/shard_map/dot_general | solution.py:56
  172.7 4.9 %fusion.4 = bf16[288,2048]{1,0:T(8,128)(2,1)S(1)} fusion(f32[288,2048]{1,0:T(8,128)S(1)} %fusion.47, bf16[288,1408]{1,0:T(8,128)(2,1)} %get-tuple-element.40, bf16[2048,1408]{1,0:T(8,128)(2,1)} %constant_dynamic-update-slice_fusion.8), kind=kOutput, calls=%fused_computation.14 | convolution fusion | flops 1662124032 | bytes 10117120 | tf_op jit(solution)/shard_map/dot_general | solution.py:56
  178.9 9.0 %all-to-all-done.1 = bf16[8,36,2048]{2,1,0:T(8,128)(2,1)} async-done(((bf16[8,36,2048]{2,1,0:T(8,128)(2,1)}), bf16[8,36,2048]{2,1,0:T(8,128)(2,1)}, u32[]{:S(2)}, u32[]{:S(2)}) %all-to-all-start.1) | async-done | bytes 1179680 | tf_op jit(solution)/shard_map/all_to_all | solution.py:91
  187.9 3.8 %all-to-all-start.3 = ((bf16[8,36,2048]{2,1,0:T(8,128)(2,1)}), bf16[8,36,2048]{2,1,0:T(8,128)(2,1)S(1)}, u32[]{:S(2)}, u32[]{:S(2)}) async-start(bf16[8,36,2048]{2,1,0:T(8,128)(2,1)} %reshape.55), calls=%async_computation.3 | async-start | bytes 2621440 | tf_op jit(solution)/shard_map/all_to_all | solution.py:91
  192.8 19.8 %collective-permute-done.13 = bf16[288,1408]{1,0:T(8,128)(2,1)} collective-permute-done((bf16[288,1408]{1,0:T(8,128)(2,1)}, bf16[288,1408]{1,0:T(8,128)(2,1)}, u32[]{:S(2)}, u32[]{:S(2)}) %collective-permute-start.13) | collective-permute-done | bytes 811040 | tf_op jit(solution)/shard_map/ppermute | solution.py:12
  212.7 5.3 %fusion = bf16[1,1024,1408]{2,1,0:T(8,128)(2,1)} fusion(bf16[576,1024]{1,0:T(8,128)(2,1)S(1)} %constant_dynamic-update-slice_fusion.12, bf16[288,1408]{1,0:T(8,128)(2,1)} %collective-permute-done.13, bf16[288,1408]{1,0:T(8,128)(2,1)} %get-tuple-element.40), kind=kOutput, calls=%fused_computation.3 | convolution fusion | flops 1665630208 | bytes 5685248 | tf_op jit(solution)/shard_map/dot_general | solution.py:56
  218.0 11.6 %collective-permute-done.14 = bf16[288,1408]{1,0:T(8,128)(2,1)} collective-permute-done((bf16[288,1408]{1,0:T(8,128)(2,1)}, bf16[288,1408]{1,0:T(8,128)(2,1)}, u32[]{:S(2)}, u32[]{:S(2)}) %collective-permute-start.14) | collective-permute-done | bytes 811040 | tf_op jit(solution)/shard_map/ppermute | solution.py:12
  229.6 5.3 %fusion.1 = bf16[1,1024,1408]{2,1,0:T(8,128)(2,1)} fusion(bf16[576,1024]{1,0:T(8,128)(2,1)S(1)} %constant_dynamic-update-slice_fusion.12, bf16[288,1408]{1,0:T(8,128)(2,1)} %collective-permute-done.14, bf16[288,1408]{1,0:T(8,128)(2,1)} %get-tuple-element.41), kind=kOutput, calls=%fused_computation.4 | convolution fusion | flops 1665630208 | bytes 5685248 | tf_op jit(solution)/shard_map/dot_general | solution.py:56
  235.0 5.4 %fusion.2 = bf16[1,704,2048]{2,1,0:T(8,128)(2,1)} fusion(bf16[288,2048]{1,0:T(8,128)(2,1)} %collective-permute-done.16, bf16[288,2048]{1,0:T(8,128)(2,1)S(1)} %copy-done.12, bf16[288,704]{1,0:T(8,128)(2,1)} %collective-permute-done.15, bf16[288,704]{1,0:T(8,128)(2,1)S(1)} %get-tuple-element.51), kind=kOutput, calls=%fused_computation.5 | convolution fusion | flops 1668726784 | bytes 6053888 | tf_op jit(solution)/shard_map/dot_general | solution.py:56
  (113 shorter events, 54.1 us)
Async XLA Ops:
  5.4 10.9 %copy-start.3 = (bf16[1,1024,1408]{2,1,0:T(8,128)(2,1)S(1)}, bf16[1,1024,1408]{2,1,0:T(8,128)(2,1)}, u32[]{:S(2)}) copy-start(bf16[1,1024,1408]{2,1,0:T(8,128)(2,1)} %param.12) | copy-start | bytes 8650756
  7.8 11.8 %copy-start.16 = (f32[128,2]{0,1:T(2,128)S(1)}, f32[128,2]{0,1:T(2,128)}, u32[]{:S(2)}) copy-start(f32[128,2]{0,1:T(2,128)} %param.9) | copy-start | bytes 3076
  7.8 38.8 %all-to-all-start = ((bf16[8,36,2048]{2,1,0:T(8,128)(2,1)}), bf16[8,36,2048]{2,1,0:T(8,128)(2,1)}, u32[]{:S(2)}, u32[]{:S(2)}) async-start(bf16[8,36,2048]{2,1,0:T(8,128)(2,1)} %reshape.49), calls=%async_computation | async-start | bytes 2621440 | tf_op jit(solution)/shard_map/all_to_all | solution.py:91
  14.3 33.7 %collective-permute-start = (bf16[256,1408]{1,0:T(8,128)(2,1)}, bf16[256,1408]{1,0:T(8,128)(2,1)}, u32[]{:S(2)}, u32[]{:S(2)}) collective-permute-start(bf16[256,1408]{1,0:T(8,128)(2,1)} %get-tuple-element.23), channel_id=1, source_target_pairs={{0,2},{2,0},{1,3},{3,1},{4,6},{6,4},{5,7},{7,5},{8,10},{10,8},{9,1... | collective-permute-start | bytes 2162696 | tf_op jit(solution)/shard_map/ppermute | solution.py:12
  15.8 33.2 %collective-permute-start.1 = (bf16[256,1408]{1,0:T(8,128)(2,1)}, bf16[256,1408]{1,0:T(8,128)(2,1)}, u32[]{:S(2)}, u32[]{:S(2)}) collective-permute-start(bf16[256,1408]{1,0:T(8,128)(2,1)} %get-tuple-element.24), channel_id=1, source_target_pairs={{0,2},{2,0},{1,3},{3,1},{4,6},{6,4},{5,7},{7,5},{8,10},{10,8},{9,1... | collective-permute-start | bytes 2162696 | tf_op jit(solution)/shard_map/ppermute | solution.py:12
  17.6 46.9 %collective-permute-start.4 = (bf16[256,1408]{1,0:T(8,128)(2,1)}, bf16[256,1408]{1,0:T(8,128)(2,1)}, u32[]{:S(2)}, u32[]{:S(2)}) collective-permute-start(bf16[256,1408]{1,0:T(8,128)(2,1)} %get-tuple-element.43), channel_id=1, source_target_pairs={{0,2},{2,0},{1,3},{3,1},{4,6},{6,4},{5,7},{7,5},{8,10},{10,8},{9,1... | collective-permute-start | bytes 2162696 | tf_op jit(solution)/shard_map/ppermute | solution.py:12
  19.1 60.4 %collective-permute-start.5 = (bf16[256,1408]{1,0:T(8,128)(2,1)}, bf16[256,1408]{1,0:T(8,128)(2,1)}, u32[]{:S(2)}, u32[]{:S(2)}) collective-permute-start(bf16[256,1408]{1,0:T(8,128)(2,1)} %get-tuple-element.42), channel_id=1, source_target_pairs={{0,2},{2,0},{1,3},{3,1},{4,6},{6,4},{5,7},{7,5},{8,10},{10,8},{9,1... | collective-permute-start | bytes 2162696 | tf_op jit(solution)/shard_map/ppermute | solution.py:12
  49.0 45.2 %collective-permute-start.2 = (bf16[256,1408]{1,0:T(8,128)(2,1)}, bf16[256,1408]{1,0:T(8,128)(2,1)}, u32[]{:S(2)}, u32[]{:S(2)}) collective-permute-start(bf16[256,1408]{1,0:T(8,128)(2,1)} %collective-permute-done), channel_id=1, source_target_pairs={{0,16},{16,0},{1,17},{17,1},{2,18},{18,2},{3,19},{19,3},{4,20},{20... | collective-permute-start | bytes 2162696 | tf_op jit(solution)/shard_map/ppermute | solution.py:12
  53.7 29.4 %copy-start.8 = (bf16[288,2048]{1,0:T(8,128)(2,1)S(1)}, bf16[288,2048]{1,0:T(8,128)(2,1)}, u32[]{:S(2)}) copy-start(bf16[288,2048]{1,0:T(8,128)(2,1)} %fusion.3) | copy-start | bytes 3538948
  55.4 65.0 %collective-permute-start.3 = (bf16[256,1408]{1,0:T(8,128)(2,1)}, bf16[256,1408]{1,0:T(8,128)(2,1)}, u32[]{:S(2)}, u32[]{:S(2)}) collective-permute-start(bf16[256,1408]{1,0:T(8,128)(2,1)} %collective-permute-done.1), channel_id=1, source_target_pairs={{0,16},{16,0},{1,17},{17,1},{2,18},{18,2},{3,19},{19,3},{4,20},{20... | collective-permute-start | bytes 2162696 | tf_op jit(solution)/shard_map/ppermute | solution.py:12
  79.5 19.3 %collective-permute-start.6 = (bf16[256,1408]{1,0:T(8,128)(2,1)}, bf16[256,1408]{1,0:T(8,128)(2,1)}, u32[]{:S(2)}, u32[]{:S(2)}) collective-permute-start(bf16[256,1408]{1,0:T(8,128)(2,1)} %collective-permute-done.4), channel_id=1, source_target_pairs={{0,16},{16,0},{1,17},{17,1},{2,18},{18,2},{3,19},{19,3},{4,20},{20... | collective-permute-start | bytes 2162696 | tf_op jit(solution)/shard_map/ppermute | solution.py:12
  81.0 19.4 %collective-permute-start.8 = (bf16[176,2048]{1,0:T(8,128)(2,1)}, bf16[176,2048]{1,0:T(8,128)(2,1)}, u32[]{:S(2)}, u32[]{:S(2)}) collective-permute-start(bf16[176,2048]{1,0:T(8,128)(2,1)} %get-tuple-element.30), channel_id=1, source_target_pairs={{0,2},{2,0},{1,3},{3,1},{4,6},{6,4},{5,7},{7,5},{8,10},{10,8},{9,1... | collective-permute-start | bytes 2162696 | tf_op jit(solution)/shard_map/ppermute | solution.py:12
  82.5 33.3 %collective-permute-start.10 = (bf16[176,2048]{1,0:T(8,128)(2,1)}, bf16[176,2048]{1,0:T(8,128)(2,1)}, u32[]{:S(2)}, u32[]{:S(2)}) collective-permute-start(bf16[176,2048]{1,0:T(8,128)(2,1)} %get-tuple-element.31), channel_id=1, source_target_pairs={{0,2},{2,0},{1,3},{3,1},{4,6},{6,4},{5,7},{7,5},{8,10},{10,8},{9,1... | collective-permute-start | bytes 2162696 | tf_op jit(solution)/shard_map/ppermute | solution.py:12
  84.2 66.5 %all-to-all-start.2 = ((bf16[8,36,2048]{2,1,0:T(8,128)(2,1)}), bf16[8,36,2048]{2,1,0:T(8,128)(2,1)S(1)}, u32[]{:S(2)}, u32[]{:S(2)}) async-start(bf16[8,36,2048]{2,1,0:T(8,128)(2,1)} %reshape.53), calls=%async_computation.2 | async-start | bytes 2621440 | tf_op jit(solution)/shard_map/all_to_all | solution.py:91
  94.2 33.2 %collective-permute-start.7 = (bf16[256,1408]{1,0:T(8,128)(2,1)}, bf16[256,1408]{1,0:T(8,128)(2,1)S(1)}, u32[]{:S(2)}, u32[]{:S(2)}) collective-permute-start(bf16[256,1408]{1,0:T(8,128)(2,1)} %collective-permute-done.5), channel_id=1, source_target_pairs={{0,16},{16,0},{1,17},{17,1},{2,18},{18,2},{3,19},{19,3},{4,20},{20... | collective-permute-start | bytes 2162696 | tf_op jit(solution)/shard_map/ppermute | solution.py:12
  98.8 61.1 %collective-permute-start.12 = (bf16[288,1024]{1,0:T(8,128)(2,1)}, bf16[288,1024]{1,0:T(8,128)(2,1)}, u32[]{:S(2)}, u32[]{:S(2)}) collective-permute-start(bf16[288,1024]{1,0:T(8,128)(2,1)} %get-tuple-element.49), channel_id=1, source_target_pairs={{0,2},{2,0},{1,3},{3,1},{4,6},{6,4},{5,7},{7,5},{8,10},{10,8},{9,1... | collective-permute-start | bytes 1769480 | tf_op jit(solution)/shard_map/ppermute | solution.py:12
  100.4 32.9 %collective-permute-start.9 = (bf16[176,2048]{1,0:T(8,128)(2,1)}, bf16[176,2048]{1,0:T(8,128)(2,1)S(1)}, u32[]{:S(2)}, u32[]{:S(2)}) collective-permute-start(bf16[176,2048]{1,0:T(8,128)(2,1)} %collective-permute-done.8), channel_id=1, source_target_pairs={{0,16},{16,0},{1,17},{17,1},{2,18},{18,2},{3,19},{19,3},{4,20},{20... | collective-permute-start | bytes 2162696 | tf_op jit(solution)/shard_map/ppermute | solution.py:12
  115.8 28.0 %collective-permute-start.11 = (bf16[176,2048]{1,0:T(8,128)(2,1)}, bf16[176,2048]{1,0:T(8,128)(2,1)S(1)}, u32[]{:S(2)}, u32[]{:S(2)}) collective-permute-start(bf16[176,2048]{1,0:T(8,128)(2,1)} %collective-permute-done.10), channel_id=1, source_target_pairs={{0,16},{16,0},{1,17},{17,1},{2,18},{18,2},{3,19},{19,3},{4,20},{20... | collective-permute-start | bytes 2162696 | tf_op jit(solution)/shard_map/ppermute | solution.py:12
  120.4 6.9 %slice-start = ((s8[5767168]{0:T(1024)(128)(4,1)}), s8[4194304]{0:T(1024)(128)(4,1)S(1)}, s32[]{:S(2)}) async-start(s8[5767168]{0:T(1024)(128)(4,1)} %bitcast.52), calls=%async_computation.4 | async-start | bytes 8388608
  122.6 4.8 %slice-start.1 = ((s8[5767168]{0:T(1024)(128)(4,1)}), s8[1572864]{0:T(1024)(128)(4,1)S(1)}, s32[]{:S(2)}) async-start(s8[5767168]{0:T(1024)(128)(4,1)} %bitcast.52), calls=%async_computation.5 | async-start | bytes 3145728
  131.0 13.8 %copy-start.13 = (bf16[288,1408]{1,0:T(8,128)(2,1)}, bf16[288,1408]{1,0:T(8,128)(2,1)S(1)}, u32[]{:S(2)}) copy-start(bf16[288,1408]{1,0:T(8,128)(2,1)S(1)} %get-tuple-element.32) | copy-start | bytes 2433028
  150.7 4.9 %copy-start.14 = (bf16[288,1408]{1,0:T(8,128)(2,1)S(1)}, bf16[288,1408]{1,0:T(8,128)(2,1)}, u32[]{:S(2)}) copy-start(bf16[288,1408]{1,0:T(8,128)(2,1)} %copy-done.13) | copy-start | bytes 2433028
  150.7 37.2 %all-to-all-start.1 = ((bf16[8,36,2048]{2,1,0:T(8,128)(2,1)}), bf16[8,36,2048]{2,1,0:T(8,128)(2,1)}, u32[]{:S(2)}, u32[]{:S(2)}) async-start(bf16[8,36,2048]{2,1,0:T(8,128)(2,1)} %reshape.51), calls=%async_computation.1 | async-start | bytes 2621440 | tf_op jit(solution)/shard_map/all_to_all | solution.py:91
  156.7 78.3 %collective-permute-start.15 = (bf16[288,704]{1,0:T(8,128)(2,1)}, bf16[288,704]{1,0:T(8,128)(2,1)}, u32[]{:S(2)}, u32[]{:S(2)}) collective-permute-start(bf16[288,704]{1,0:T(8,128)(2,1)} %get-tuple-element.52), channel_id=1, source_target_pairs={{0,2},{2,0},{1,3},{3,1},{4,6},{6,4},{5,7},{7,5},{8,10},{10,8},{9,1... | collective-permute-start | bytes 1216520 | tf_op jit(solution)/shard_map/ppermute | solution.py:12
  158.3 11.2 %slice-start.2 = ((s8[5767168]{0:T(1024)(128)(4,1)}), s8[1572864]{0:T(1024)(128)(4,1)S(1)}, s32[]{:S(2)}) async-start(s8[5767168]{0:T(1024)(128)(4,1)} %bitcast.54), calls=%async_computation.6 | async-start | bytes 3145728
  159.4 75.6 %collective-permute-start.16 = (bf16[288,2048]{1,0:T(8,128)(2,1)}, bf16[288,2048]{1,0:T(8,128)(2,1)}, u32[]{:S(2)}, u32[]{:S(2)}) collective-permute-start(bf16[288,2048]{1,0:T(8,128)(2,1)} %reshape.54), channel_id=1, source_target_pairs={{0,2},{2,0},{1,3},{3,1},{4,6},{6,4},{5,7},{7,5},{8,10},{10,8},{9,1... | collective-permute-start | bytes 3538952 | tf_op jit(solution)/shard_map/ppermute | solution.py:12
  159.9 9.6 %slice-start.3 = ((s8[5767168]{0:T(1024)(128)(4,1)}), s8[4194304]{0:T(1024)(128)(4,1)S(1)}, s32[]{:S(2)}) async-start(s8[5767168]{0:T(1024)(128)(4,1)} %bitcast.54), calls=%async_computation.7 | async-start | bytes 8388608
  167.5 45.2 %collective-permute-start.13 = (bf16[288,1408]{1,0:T(8,128)(2,1)}, bf16[288,1408]{1,0:T(8,128)(2,1)}, u32[]{:S(2)}, u32[]{:S(2)}) collective-permute-start(bf16[288,1408]{1,0:T(8,128)(2,1)} %get-tuple-element.40), channel_id=1, source_target_pairs={{0,2},{2,0},{1,3},{3,1},{4,6},{6,4},{5,7},{7,5},{8,10},{10,8},{9,1... | collective-permute-start | bytes 2433032 | tf_op jit(solution)/shard_map/ppermute | solution.py:12
  169.0 60.7 %collective-permute-start.14 = (bf16[288,1408]{1,0:T(8,128)(2,1)}, bf16[288,1408]{1,0:T(8,128)(2,1)}, u32[]{:S(2)}, u32[]{:S(2)}) collective-permute-start(bf16[288,1408]{1,0:T(8,128)(2,1)} %get-tuple-element.41), channel_id=1, source_target_pairs={{0,2},{2,0},{1,3},{3,1},{4,6},{6,4},{5,7},{7,5},{8,10},{10,8},{9,1... | collective-permute-start | bytes 2433032 | tf_op jit(solution)/shard_map/ppermute | solution.py:12
  177.6 14.0 %copy-start.11 = (bf16[288,1024]{1,0:T(8,128)(2,1)S(1)}, bf16[288,1024]{1,0:T(8,128)(2,1)}, u32[]{:S(2)}) copy-start(bf16[288,1024]{1,0:T(8,128)(2,1)} %get-tuple-element.36) | copy-start | bytes 1769476
  187.9 56.6 %all-to-all-start.3 = ((bf16[8,36,2048]{2,1,0:T(8,128)(2,1)}), bf16[8,36,2048]{2,1,0:T(8,128)(2,1)S(1)}, u32[]{:S(2)}, u32[]{:S(2)}) async-start(bf16[8,36,2048]{2,1,0:T(8,128)(2,1)} %reshape.55), calls=%async_computation.3 | async-start | bytes 2621440 | tf_op jit(solution)/shard_map/all_to_all | solution.py:91
  218.0 17.0 %copy-start.12 = (bf16[288,2048]{1,0:T(8,128)(2,1)S(1)}, bf16[288,2048]{1,0:T(8,128)(2,1)}, u32[]{:S(2)}) copy-start(bf16[288,2048]{1,0:T(8,128)(2,1)} %reshape.54) | copy-start | bytes 3538948
  (11 other events, 33.9 us)
